TPU v7x, 256 devices: a whole 4x4x8 slice. The times are simulated.
256 devices in a mesh: grp: 2 (over z_lo), seq: 16 (over z_hi, x), dp: 8 (over y, core).
Axes of the slice: x: 4, y: 4, z: 8 (z_hi: 4, z_lo: 2; z = z_hi * 2 + z_lo), core: 2. Of those that a mesh axis runs over, the one named last changes fastest.
Arguments:
- features: bfloat16 [16, 8, 16, 16, 512], P(('grp', 'dp'), None, 'seq'), may hold values from -6 to 6
- conv_weight: bfloat16 [3, 3, 512, 4], replicated, may hold values from -0.09375 to 0.09375
- conv_bias: float32 [4], replicated, may hold values from -3 to 3
- noise: bfloat16 [16, 8, 16, 16, 4], P(('grp', 'dp'), None, 'seq'), may hold values from -6 to 6
- timestep: int32 [16], P(('grp', 'dp')), may hold values from 0 to 999
- camera: int32 [16, 8], P(('grp', 'dp')), may hold values from 0 to 63
- view_table: bfloat16 [64, 1152], replicated, may hold values from -6 to 6
- latent_proj: bfloat16 [4, 1152], replicated, may hold values from -3 to 3
- hidden: bfloat16 [16, 8, 16, 16, 1152], P(('grp', 'dp'), None, 'seq'), may hold values from -8 to 8
- ln_gain: float32 [1152], replicated, may hold values from 0.1 to 1.9
- qkv_weight: bfloat16 [1152, 3456], replicated, may hold values from -1 to 1
- cotangent: bfloat16 [16, 8, 16, 16, 1152], P(('grp', 'dp'), None, None, None, 'seq'), may hold values from -6 to 6
Outputs:
- attended: bfloat16 [16, 8, 16, 16, 1152], P(('grp', 'dp'), None, None, None, 'seq')
- hidden_grad: bfloat16 [16, 8, 16, 16, 1152], P(('grp', 'dp'), None, 'seq')
- weight_grad: float32 [16, 1152, 216], P('seq', ('grp', 'dp'))
All inputs are finite; a program needn't handle non-finite values.
Results may differ from a plain program's by a relative error of at most 0.022.
Values may be sent and summed in bfloat16 or wider, within the bound.
A program may use at most 192 MiB of HBM per device.

v0:
```python
import math

import jax
import jax.numpy as jnp
from jax import lax
from jax.sharding import PartitionSpec as P

H = 16
TSTEPS = 1000


def padded_2(block, sides, width):
    for axis, dim in sides:
        count = lax.axis_size(axis)
        forward = [(i, i + 1) for i in range(count - 1)]
        backward = [(target, source) for source, target in forward]
        low = lax.ppermute(
            lax.slice_in_dim(block, block.shape[dim] - width, None, axis=dim), axis, forward
        )
        high = lax.ppermute(lax.slice_in_dim(block, 0, width, axis=dim), axis, backward)
        block = jnp.concatenate([low, block, high], axis=dim)
    return block


def encode_latent(rimmed, conv_weight, conv_bias):
    activated = jax.nn.silu(rimmed.astype(jnp.float32))
    padded = jnp.pad(activated, ((0, 0), (0, 0), (0, 0), (1, 1), (0, 0)))
    rows_out = padded.shape[2] - 2
    cols_out = padded.shape[3] - 2
    latent = jnp.zeros(padded.shape[:2] + (rows_out, cols_out, conv_weight.shape[3]), jnp.float32)
    latent = latent + conv_bias
    for row_tap in range(3):
        for col_tap in range(3):
            window = padded[:, :, row_tap : row_tap + rows_out, col_tap : col_tap + cols_out, :]
            latent = latent + jnp.einsum(
                "svhwc,co->svhwo",
                window,
                conv_weight[row_tap, col_tap].astype(jnp.float32),
                precision=lax.Precision.HIGHEST,
            )
    return latent


def layer_input(latent, noise, timestep, camera, view_table, latent_proj, hidden):
    level = timestep.astype(jnp.float32) / TSTEPS
    signal = jnp.cos((level + 0.008) / 1.008 * (math.pi / 2.0)) ** 2
    keep_scale = jnp.sqrt(signal)[:, None, None, None, None]
    noise_scale = jnp.sqrt(1.0 - signal)[:, None, None, None, None]
    noisy = keep_scale * latent + noise_scale * noise.astype(jnp.float32)
    onehot = (camera[..., None] == jnp.arange(view_table.shape[0], dtype=jnp.int32)).astype(
        jnp.float32
    )
    view_embed = jnp.einsum(
        "svn,nd->svd", onehot, view_table.astype(jnp.float32), precision=lax.Precision.HIGHEST
    )
    injected = jnp.einsum(
        "svhwc,cd->svhwd", noisy, latent_proj.astype(jnp.float32), precision=lax.Precision.HIGHEST
    )
    return hidden.astype(jnp.float32) + injected + view_embed[:, :, None, None, :]


def normalize(inputs, ln_gain):
    mean_value = jnp.mean(inputs, -1, keepdims=True)
    centered = inputs - mean_value
    variance = jnp.mean(centered * centered, -1, keepdims=True)
    inverse = lax.rsqrt(variance + 1e-06)
    unit = centered * inverse
    return (unit, inverse, (unit * ln_gain).astype(jnp.bfloat16))


def norm_backward(normed_grad, unit, inverse, ln_gain):
    scaled = normed_grad * ln_gain
    first = jnp.mean(scaled, -1, keepdims=True)
    second = jnp.mean(scaled * unit, -1, keepdims=True)
    return inverse * (scaled - first - unit * second)


def attend(queries, keys, values, upstream):
    count = queries.shape[0]
    block = min(512, count)
    nblocks = count // block
    scale = keys.shape[1] ** (-0.5)

    def step(carry, item):
        key_grad, value_grad = carry
        query_block, up_block = item
        scores = jnp.dot(query_block, keys.T, preferred_element_type=jnp.float32) * scale
        highest = jnp.max(scores, -1, keepdims=True)
        weights = jnp.exp(scores - highest)
        probs = weights / jnp.sum(weights, -1, keepdims=True)
        probs_low = probs.astype(jnp.bfloat16)
        output = jnp.dot(probs_low, values, preferred_element_type=jnp.float32).astype(jnp.bfloat16)
        prob_grad = jnp.dot(up_block, values.T, preferred_element_type=jnp.float32)
        row_total = jnp.sum(probs * prob_grad, -1, keepdims=True)
        score_grad = (probs * (prob_grad - row_total) * scale).astype(jnp.bfloat16)
        query_grad = jnp.dot(score_grad, keys, preferred_element_type=jnp.float32)
        key_grad = key_grad + jnp.dot(score_grad.T, query_block, preferred_element_type=jnp.float32)
        value_grad = value_grad + jnp.dot(probs_low.T, up_block, preferred_element_type=jnp.float32)
        return ((key_grad, value_grad), (output, query_grad))

    zeros = jnp.zeros(keys.shape, jnp.float32)
    blocks_in = (queries.reshape(nblocks, block, -1), upstream.reshape(nblocks, block, -1))
    (key_grad, value_grad), (outputs, query_grads) = lax.scan(step, (zeros, zeros), blocks_in)
    return (outputs.reshape(count, -1), query_grads.reshape(count, -1), key_grad, value_grad)


def per_head(item):
    triple, upstream = item
    return attend(triple[0], triple[1], triple[2], upstream)


def on_device(
    features,
    conv_weight,
    conv_bias,
    noise,
    timestep,
    camera,
    view_table,
    latent_proj,
    hidden,
    ln_gain,
    qkv_weight,
    cotangent,
):
    rimmed = padded_2(features, (("seq", 2),), 1)
    latent = encode_latent(rimmed, conv_weight, conv_bias)
    inputs = layer_input(latent, noise, timestep, camera, view_table, latent_proj, hidden)
    unit, inverse, normed = normalize(inputs, ln_gain)
    scenes, views, rows, cols, width = hidden.shape
    head_size = width // H
    flat_normed = normed.reshape(-1, width)
    projected = jnp.dot(flat_normed, qkv_weight, preferred_element_type=jnp.float32).astype(
        jnp.bfloat16
    )
    projected = projected.reshape(scenes, views, rows, cols, 3, H, head_size)
    by_head = lax.all_to_all(projected, "seq", split_axis=5, concat_axis=2, tiled=True)
    all_rows = by_head.shape[2]
    local_heads = by_head.shape[5]
    count = views * all_rows * cols
    triples = by_head.transpose(0, 5, 4, 1, 2, 3, 6).reshape(
        scenes * local_heads, 3, count, head_size
    )
    upstream = cotangent.reshape(scenes, count, local_heads, head_size).transpose(0, 2, 1, 3)
    upstream = upstream.reshape(scenes * local_heads, count, head_size)
    outputs, query_grad, key_grad, value_grad = lax.map(per_head, (triples, upstream))
    attended = (
        outputs.reshape(scenes, local_heads, count, head_size)
        .transpose(0, 2, 1, 3)
        .reshape(cotangent.shape)
    )
    stacked_grads = jnp.stack([query_grad, key_grad, value_grad], 1).astype(jnp.bfloat16)
    head_layout = stacked_grads.reshape(scenes, local_heads, 3, views, all_rows, cols, head_size)
    head_grads = head_layout.transpose(0, 3, 4, 5, 2, 1, 6)
    token_grads = lax.all_to_all(head_grads, "seq", split_axis=2, concat_axis=5, tiled=True)
    flat_grads = token_grads.reshape(-1, 3 * width)
    groups = lax.axis_size("grp")
    datas = lax.axis_size("dp")
    row_block = width // (groups * datas)
    head_term = jnp.einsum(
        "svrcd,sltvrce->ldte",
        lax.all_gather(normed, "seq", axis=2, tiled=True),
        head_layout,
        preferred_element_type=jnp.float32,
    )
    weight_grad = (
        lax.psum_scatter(
            head_term.astype(jnp.bfloat16), ("grp", "dp"), scatter_dimension=1, tiled=True
        )
        .astype(jnp.float32)
        .reshape(local_heads, row_block, 3 * head_size)
    )
    normed_grad = jnp.dot(flat_grads, qkv_weight.T, preferred_element_type=jnp.float32).reshape(
        inputs.shape
    )
    hidden_grad = norm_backward(normed_grad, unit, inverse, ln_gain).astype(jnp.bfloat16)
    return (attended, hidden_grad, weight_grad)


def solution(mesh):
    return jax.shard_map(
        on_device,
        mesh=mesh,
        in_specs=(
            P(("grp", "dp"), None, "seq", None, None),
            P(),
            P(),
            P(("grp", "dp"), None, "seq", None, None),
            P(("grp", "dp")),
            P(("grp", "dp"), None),
            P(),
            P(),
            P(("grp", "dp"), None, "seq", None, None),
            P(),
            P(),
            P(("grp", "dp"), None, None, None, "seq"),
        ),
        out_specs=(
            P(("grp", "dp"), None, None, None, "seq"),
            P(("grp", "dp"), None, "seq", None, None),
            P("seq", ("grp", "dp"), None),
        ),
        check_vma=False,
    )
```

profile of v0, /device:TPU:4, one launch (start us, length us, event | category | flops | bytes accessed | tf_op | source)
XLA Modules:
  0.0 289.2 jit_solution(1019398355988941391)
XLA Ops:
  7.2 3.2 %collective-permute-start = (bf16[1,8,1,16,512]{4,3,1,2,0:T(8,128)(2,1)}, bf16[1,8,1,16,512]{4,3,1,2,0:T(8,128)(2,1)S(1)}, u32[]{:S(2)}, u32[]{:S(2)}) collective-permute-start(bf16[1,8,1,16,512]{4,3,1,2,0:T(8,128)(2,1)} %bitcast.246), channel_id=1, source_target_pairs={{0,8},{8,16},{16,24},{24,32},{32,40},{40,48},{48,56},{56,64},{64,7... | collective-permute-start | bytes 393224 | tf_op jit(solution)/shard_map/ppermute | solution.py:17
  10.5 2.7 collective-permute-start.1
  14.9 4.1 %collective-permute-done.1 = bf16[1,8,1,16,512]{4,3,1,2,0:T(8,128)(2,1)S(1)} collective-permute-done((bf16[1,8,1,16,512]{4,3,1,2,0:T(8,128)(2,1)}, bf16[1,8,1,16,512]{4,3,1,2,0:T(8,128)(2,1)S(1)}, u32[]{:S(2)}, u32[]{:S(2)}) %collective-permute-start.1) | collective-permute-done | bytes 131104 | tf_op jit(solution)/shard_map/ppermute | solution.py:20
  20.1 1.4 convolution_add_fusion.10
  21.5 1.6 convolution_add_fusion.9
  30.7 1.3 fusion.47
  33.1 2.3 convolution_convert_fusion.1
  35.4 4.0 %reshape.326 = bf16[1,8,1,16,3,16,72]{6,5,4,3,1,2,0:T(8,128)(2,1)S(1)} reshape(bf16[128,3456]{1,0:T(8,128)(2,1)} %convolution_convert_fusion.1) | data formatting | bytes 1769472 | tf_op jit(solution)/shard_map/reshape | solution.py:136
  39.4 1.6 copy.94
  41.0 15.9 %all-to-all-start = ((bf16[1,8,1,16,3,16,72]{6,3,4,2,1,0,5:T(8,128)(2,1)}), bf16[1,8,1,16,3,16,72]{6,3,4,2,1,0,5:T(8,128)(2,1)S(1)}, u32[]{:S(2)}, u32[]{:S(2)}) async-start(bf16[1,8,1,16,3,16,72]{6,3,4,2,1,0,5:T(8,128)(2,1)} %copy.94), calls=%async_computation | async-start | bytes 3145728 | tf_op jit(solution)/shard_map/all_to_all | solution.py:137
  58.1 41.3 %all-to-all-done = bf16[1,8,1,16,3,16,72]{6,3,4,2,1,0,5:T(8,128)(2,1)S(1)} async-done(((bf16[1,8,1,16,3,16,72]{6,3,4,2,1,0,5:T(8,128)(2,1)}), bf16[1,8,1,16,3,16,72]{6,3,4,2,1,0,5:T(8,128)(2,1)S(1)}, u32[]{:S(2)}, u32[]{:S(2)}) %all-to-all-start) | async-done | bytes 884768 | tf_op jit(solution)/shard_map/all_to_all | solution.py:137
  99.9 57.9 %while.30 = (s32[]{:T(128)}, f32[2048,72]{0,1:T(8,128)}, f32[2048,72]{0,1:T(8,128)S(1)}, bf16[4,512,72]{1,2,0:T(8,128)(2,1)}, bf16[4,512,72]{1,2,0:T(8,128)(2,1)...) while((s32[]{:T(128)}, f32[2048,72]{0,1:T(8,128)}, ...), condition=%wide.region_6.7_spmd.clone, body=%wide.region_2.6_spmd.clone.sunk | while | flops 923372032 | bytes 87073576 | solution.py:103
  101.6 2.2 multiply_reduce_fusion.6
  103.8 2.0 copy-done.1
  106.4 2.4 convolution_add_fusion.13
  108.8 1.4 fusion.135
  110.2 1.5 convolution_add_fusion.14
  111.8 2.5 fusion.134
  115.9 2.2 multiply_reduce_fusion.6
  118.2 2.0 copy-done.1
  120.8 2.6 convolution_add_fusion.13
  123.4 1.4 fusion.135
  124.8 1.6 convolution_add_fusion.14
  126.3 2.5 fusion.134
  130.4 2.2 multiply_reduce_fusion.6
  132.7 2.0 copy-done.1
  135.3 2.7 convolution_add_fusion.13
  137.9 1.4 fusion.135
  139.3 1.5 convolution_add_fusion.14
  140.9 2.5 fusion.134
  145.0 2.2 multiply_reduce_fusion.6
  147.3 2.0 copy-done.1
  149.8 2.6 convolution_add_fusion.13
  152.5 1.4 fusion.135
  153.8 1.5 convolution_add_fusion.14
  155.4 2.5 fusion.134
  159.1 1.3 copy.100
  161.1 1.6 copy.102
  162.8 7.1 %all-to-all-start.1 = ((bf16[1,8,16,16,3,1,72]{6,3,1,4,5,0,2:T(8,128)(2,1)}), bf16[1,8,16,16,3,1,72]{6,3,1,4,5,0,2:T(8,128)(2,1)S(1)}, u32[]{:S(2)}, u32[]{:S(2)}) async-start(bf16[1,8,16,16,3,1,72]{6,3,1,4,5,0,2:T(8,128)(2,1)} %copy.102), calls=%async_computation.1 | async-start | bytes 3145728 | tf_op jit(solution)/shard_map/all_to_all | solution.py:155
  172.0 2.0 copy.106
  174.0 2.0 copy.98
  176.0 27.9 %all-to-all-done.1 = bf16[1,8,16,16,3,1,72]{6,3,1,4,5,0,2:T(8,128)(2,1)S(1)} async-done(((bf16[1,8,16,16,3,1,72]{6,3,1,4,5,0,2:T(8,128)(2,1)}), bf16[1,8,16,16,3,1,72]{6,3,1,4,5,0,2:T(8,128)(2,1)S(1)}, u32[]{:S(2)}, u32[]{:S(2)}) %all-to-all-start.1) | async-done | bytes 884768 | tf_op jit(solution)/shard_map/all_to_all | solution.py:155
  203.9 2.2 copy.103
  206.0 3.0 %dot_general.77 = bf16[8,16,3456]{2,1,0:T(8,128)(2,1)S(1)} reshape(bf16[1,8,1,16,3,16,1,72]{7,5,4,3,1,6,2,0:T(8,128)(2,1)} %copy.103) | data formatting | bytes 1769472 | tf_op jit(solution)/shard_map/dot_general | solution.py:173
  209.1 8.0 %fusion.36 = bf16[1,1152,3,72]{1,3,2,0:T(8,128)(2,1)S(1)} fusion(bf16[8,16,16,1152,1]{3,2,0,1,4:T(8,128)(2,1)} %bitcast.250, bf16[1,8,16,16,72]{4,2,1,0,3:T(8,128)(2,1)} %copy.106, bf16[1,8,16,16,72]{4,2,1,0,3:T(8,128)(2,1)S(1)} %copy-done.12, bf16[1,8,16,16,72]{4,2,1,0,3:T(8,128)(2,1)S(1)} %copy-done.11), kind=kOutput, calls=%fused_computation.40 | convolution fusion | flops 1020349440 | bytes 6100992 | tf_op jit(solution)/shard_map/svrcd,sltvrce->ldte/dot_general | solution.py:160
  218.0 1.3 reshape.346
  219.3 5.8 %fusion.51 = (f32[8,16]{1,0:T(8,128)S(1)}, f32[8,16,1152]{2,1,0:T(8,128)S(1)}) fusion(f32[1,8,1,16,1152]{4,3,1,2,0:T(8,128)S(1)} %copy-done.5, f32[8,16]{1,0:T(8,128)S(1)} %add_rsqrt_fusion, f32[8,16]{1,0:T(8,128)S(1)} %broadcast_multiply_fusion.2, f32[1152]{0:T(1024)S(1)} %copy-done.14, bf16[8,16,3456]{2,1,0:T(8,128)(2,1)S(1)} %dot_general.77, ...), kind=kOutput, calls=%fused_computation.72 | convolution fusion | flops 1019953024 | bytes 10033152 | tf_op jit(solution)/shard_map/dot_general | solution.py:173
  226.2 54.4 %reduce-scatter.4.cloned.1.call-done = bf16[72,216]{1,0:T(8,128)(2,1)} async-done(((bf16[1152,216]{1,0:T(8,128)(2,1)}), bf16[72,216]{1,0:T(8,128)(2,1)}) %reduce-scatter.4.cloned.1.call-update) | async-done | bytes 31120
  (119 shorter events, 28.6 us)
Async XLA Ops:
  7.2 6.9 %copy-start = (bf16[64,1152]{1,0:T(8,128)(2,1)S(1)}, bf16[64,1152]{1,0:T(8,128)(2,1)}, u32[]{:S(2)}) copy-start(bf16[64,1152]{1,0:T(8,128)(2,1)} %param.20) | copy-start | bytes 442372
  7.2 23.6 %copy-start.16 = (bf16[1,8,1,16,4]{3,4,2,1,0:T(4,128)(2,1)S(1)}, bf16[1,8,1,16,4]{3,4,2,1,0:T(4,128)(2,1)}, u32[]{:S(2)}) copy-start(bf16[1,8,1,16,4]{3,4,2,1,0:T(4,128)(2,1)} %param.17) | copy-start | bytes 3076
  7.2 24.8 %copy-start.15 = (bf16[4,1152]{1,0:T(4,128)(2,1)S(1)}, bf16[4,1152]{1,0:T(4,128)(2,1)}, u32[]{:S(2)}) copy-start(bf16[4,1152]{1,0:T(4,128)(2,1)} %param.21) | copy-start | bytes 27652
  7.2 24.8 %copy-start.13 = (bf16[1,8,1,16,1152]{4,3,2,1,0:T(8,128)(2,1)S(1)}, bf16[1,8,1,16,1152]{4,3,2,1,0:T(8,128)(2,1)}, u32[]{:S(2)}) copy-start(bf16[1,8,1,16,1152]{4,3,2,1,0:T(8,128)(2,1)} %param.22) | copy-start | bytes 884740
  7.2 7.7 %collective-permute-start = (bf16[1,8,1,16,512]{4,3,1,2,0:T(8,128)(2,1)}, bf16[1,8,1,16,512]{4,3,1,2,0:T(8,128)(2,1)S(1)}, u32[]{:S(2)}, u32[]{:S(2)}) collective-permute-start(bf16[1,8,1,16,512]{4,3,1,2,0:T(8,128)(2,1)} %bitcast.246), channel_id=1, source_target_pairs={{0,8},{8,16},{16,24},{24,32},{32,40},{40,48},{48,56},{56,64},{64,7... | collective-permute-start | bytes 393224 | tf_op jit(solution)/shard_map/ppermute | solution.py:17
  10.5 8.5 %collective-permute-start.1 = (bf16[1,8,1,16,512]{4,3,1,2,0:T(8,128)(2,1)}, bf16[1,8,1,16,512]{4,3,1,2,0:T(8,128)(2,1)S(1)}, u32[]{:S(2)}, u32[]{:S(2)}) collective-permute-start(bf16[1,8,1,16,512]{4,3,1,2,0:T(8,128)(2,1)} %bitcast.247), channel_id=1, source_target_pairs={{8,0},{16,8},{24,16},{32,24},{40,32},{48,40},{56,48},{64,56},{72,6... | collective-permute-start | bytes 393224 | tf_op jit(solution)/shard_map/ppermute | solution.py:20
  14.9 18.0 %copy-start.14 = (f32[1152]{0:T(1024)S(1)}, f32[1152]{0:T(1024)}, u32[]{:S(2)}) copy-start(f32[1152]{0:T(1024)} %param.23) | copy-start | bytes 13828
  20.1 13.0 %copy-start.3 = (bf16[1152,3456]{1,0:T(8,128)(2,1)S(1)}, bf16[1152,3456]{1,0:T(8,128)(2,1)}, u32[]{:S(2)}) copy-start(bf16[1152,3456]{1,0:T(8,128)(2,1)} %param.24) | copy-start | bytes 23887876
  32.7 24.5 %copy-start.4 = (f32[1,8,1,16,1152]{4,3,1,2,0:T(8,128)}, f32[1,8,1,16,1152]{4,3,1,2,0:T(8,128)S(1)}, u32[]{:S(2)}) copy-start(f32[1,8,1,16,1152]{4,3,1,2,0:T(8,128)S(1)} %get-tuple-element.150) | copy-start | bytes 1769476
  41.0 58.4 %all-to-all-start = ((bf16[1,8,1,16,3,16,72]{6,3,4,2,1,0,5:T(8,128)(2,1)}), bf16[1,8,1,16,3,16,72]{6,3,4,2,1,0,5:T(8,128)(2,1)S(1)}, u32[]{:S(2)}, u32[]{:S(2)}) async-start(bf16[1,8,1,16,3,16,72]{6,3,4,2,1,0,5:T(8,128)(2,1)} %copy.94), calls=%async_computation | async-start | bytes 3145728 | tf_op jit(solution)/shard_map/all_to_all | solution.py:137
  56.9 152.2 %all-gather.2.cloned.1.call-start = ((), (), s32[]{:S(2)}) async-start(), calls=%async_computation.3 | async-start | bytes 5013504 | tf_op jit(solution)/shard_map/all_gather | solution.py:162
  99.9 1.6 copy-start.8
  100.0 1.6 copy-start.6
  103.8 2.0 copy-start.1
  106.4 3.8 %copy-start.2 = (f32[512,2048]{1,0:T(8,128)S(1)}, f32[512,2048]{1,0:T(8,128)}, u32[]{:S(2)}) copy-start(f32[512,2048]{1,0:T(8,128)} %copy-done.1) | copy-start | bytes 12582916 | tf_op jit(solution)/shard_map/while/body/eval_jaxpr/while
  110.2 4.0 %copy-start.7 = (bf16[2048,72]{1,0:T(8,128)(2,1)S(1)}, bf16[2048,72]{1,0:T(8,128)(2,1)}, u32[]{:S(2)}) copy-start(bf16[2048,72]{1,0:T(8,128)(2,1)} %copy-done.6) | copy-start | bytes 884740 | tf_op jit(solution)/shard_map/while/body/eval_jaxpr/while
  110.2 4.0 %copy-start.9 = (bf16[4,512,72]{2,1,0:T(8,128)(2,1)S(1)}, bf16[4,512,72]{2,1,0:T(8,128)(2,1)}, u32[]{:S(2)}) copy-start(bf16[4,512,72]{2,1,0:T(8,128)(2,1)} %copy-done.8) | copy-start | bytes 884740 | tf_op jit(solution)/shard_map/while/body/eval_jaxpr/while
  114.3 1.6 copy-start.8
  114.3 1.6 copy-start.6
  118.2 2.0 copy-start.1
  120.7 4.0 %copy-start.2 = (f32[512,2048]{1,0:T(8,128)S(1)}, f32[512,2048]{1,0:T(8,128)}, u32[]{:S(2)}) copy-start(f32[512,2048]{1,0:T(8,128)} %copy-done.1) | copy-start | bytes 12582916 | tf_op jit(solution)/shard_map/while/body/eval_jaxpr/while
  124.8 4.0 %copy-start.7 = (bf16[2048,72]{1,0:T(8,128)(2,1)S(1)}, bf16[2048,72]{1,0:T(8,128)(2,1)}, u32[]{:S(2)}) copy-start(bf16[2048,72]{1,0:T(8,128)(2,1)} %copy-done.6) | copy-start | bytes 884740 | tf_op jit(solution)/shard_map/while/body/eval_jaxpr/while
  124.8 4.0 %copy-start.9 = (bf16[4,512,72]{2,1,0:T(8,128)(2,1)S(1)}, bf16[4,512,72]{2,1,0:T(8,128)(2,1)}, u32[]{:S(2)}) copy-start(bf16[4,512,72]{2,1,0:T(8,128)(2,1)} %copy-done.8) | copy-start | bytes 884740 | tf_op jit(solution)/shard_map/while/body/eval_jaxpr/while
  128.8 1.6 copy-start.8
  128.8 1.6 copy-start.6
  132.7 2.0 copy-start.1
  135.3 4.1 %copy-start.2 = (f32[512,2048]{1,0:T(8,128)S(1)}, f32[512,2048]{1,0:T(8,128)}, u32[]{:S(2)}) copy-start(f32[512,2048]{1,0:T(8,128)} %copy-done.1) | copy-start | bytes 12582916 | tf_op jit(solution)/shard_map/while/body/eval_jaxpr/while
  139.3 4.0 %copy-start.7 = (bf16[2048,72]{1,0:T(8,128)(2,1)S(1)}, bf16[2048,72]{1,0:T(8,128)(2,1)}, u32[]{:S(2)}) copy-start(bf16[2048,72]{1,0:T(8,128)(2,1)} %copy-done.6) | copy-start | bytes 884740 | tf_op jit(solution)/shard_map/while/body/eval_jaxpr/while
  139.3 4.0 %copy-start.9 = (bf16[4,512,72]{2,1,0:T(8,128)(2,1)S(1)}, bf16[4,512,72]{2,1,0:T(8,128)(2,1)}, u32[]{:S(2)}) copy-start(bf16[4,512,72]{2,1,0:T(8,128)(2,1)} %copy-done.8) | copy-start | bytes 884740 | tf_op jit(solution)/shard_map/while/body/eval_jaxpr/while
  143.4 1.6 copy-start.8
  143.4 1.6 copy-start.6
  147.2 2.0 copy-start.1
  149.8 4.0 %copy-start.2 = (f32[512,2048]{1,0:T(8,128)S(1)}, f32[512,2048]{1,0:T(8,128)}, u32[]{:S(2)}) copy-start(f32[512,2048]{1,0:T(8,128)} %copy-done.1) | copy-start | bytes 12582916 | tf_op jit(solution)/shard_map/while/body/eval_jaxpr/while
  153.8 4.0 %copy-start.7 = (bf16[2048,72]{1,0:T(8,128)(2,1)S(1)}, bf16[2048,72]{1,0:T(8,128)(2,1)}, u32[]{:S(2)}) copy-start(bf16[2048,72]{1,0:T(8,128)(2,1)} %copy-done.6) | copy-start | bytes 884740 | tf_op jit(solution)/shard_map/while/body/eval_jaxpr/while
  153.8 4.0 %copy-start.9 = (bf16[4,512,72]{2,1,0:T(8,128)(2,1)S(1)}, bf16[4,512,72]{2,1,0:T(8,128)(2,1)}, u32[]{:S(2)}) copy-start(bf16[4,512,72]{2,1,0:T(8,128)(2,1)} %copy-done.8) | copy-start | bytes 884740 | tf_op jit(solution)/shard_map/while/body/eval_jaxpr/while
  160.7 2.0 copy-start.10
  162.8 41.1 %all-to-all-start.1 = ((bf16[1,8,16,16,3,1,72]{6,3,1,4,5,0,2:T(8,128)(2,1)}), bf16[1,8,16,16,3,1,72]{6,3,1,4,5,0,2:T(8,128)(2,1)S(1)}, u32[]{:S(2)}, u32[]{:S(2)}) async-start(bf16[1,8,16,16,3,1,72]{6,3,1,4,5,0,2:T(8,128)(2,1)} %copy.102), calls=%async_computation.1 | async-start | bytes 3145728 | tf_op jit(solution)/shard_map/all_to_all | solution.py:155
  169.9 110.8 %reduce-scatter.4.cloned.1.call-start = ((), (), s32[]{:S(2)}) async-start(), calls=%async_computation.4 | async-start | bytes 626688
  171.1 38.0 %copy-start.11 = (bf16[1,8,16,16,72]{4,2,1,0,3:T(8,128)(2,1)S(1)}, bf16[1,8,16,16,72]{4,2,1,0,3:T(8,128)(2,1)}, u32[]{:S(2)}) copy-start(bf16[1,8,16,16,72]{4,2,1,0,3:T(8,128)(2,1)} %copy.104) | copy-start | bytes 884740
  172.0 37.1 %copy-start.12 = (bf16[1,8,16,16,72]{4,2,1,0,3:T(8,128)(2,1)S(1)}, bf16[1,8,16,16,72]{4,2,1,0,3:T(8,128)(2,1)}, u32[]{:S(2)}) copy-start(bf16[1,8,16,16,72]{4,2,1,0,3:T(8,128)(2,1)} %copy.105) | copy-start | bytes 884740
  209.1 10.2 %copy-start.5 = (f32[1,8,1,16,1152]{4,3,1,2,0:T(8,128)S(1)}, f32[1,8,1,16,1152]{4,3,1,2,0:T(8,128)}, u32[]{:S(2)}) copy-start(f32[1,8,1,16,1152]{4,3,1,2,0:T(8,128)} %copy-done.4) | copy-start | bytes 1769476
Sparse Core Ops, SparseCore 0:
  60.1 99.2 all-gather.1
  219.4 61.1 reduce-scatter.3
where the time goes:
time: 290 us; the launch traced here: 289 us
  waiting for transfers between devices  128 us (44%)
  matrix products  73.6 us (25%)
  local copies, waits for them, and re-layouts  33.7 us (12%)
  starting transfers between devices  29.5 us (10%)
  between operations  15.2 us (5%)
  other arithmetic  9.26 us (3%)
    unnamed x3, waiting for transfers between devices  54.5 us
    all_to_all x1, waiting for transfers between devices, on_device(): lax.all_to_all(projected, 'seq', split_axis=5, concat_axis=2, tiled=True)  41.3 us
    all_to_all x1, waiting for transfers between devices, on_device(): lax.all_to_all(head_grads, 'seq', split_axis=2, concat_axis=5, tiled=True)  27.9 us
    all_to_all x1, starting transfers between devices, on_device(): lax.all_to_all(projected, 'seq', split_axis=5, concat_axis=2, tiled=True)  15.9 us
    dot_general x9, matrix products, encode_latent(): jnp.einsum('svhwc,co->svhwo', window, conv_weight[row_tap, col_tap].astyp...  11.9 us
    dot_general x4, matrix products, step(): jnp.dot(score_grad.T, query_block, preferred_element_type=jnp.float32)  10.3 us
    dot_general x4, matrix products, step(): jnp.dot(probs_low, values, preferred_element_type=jnp.float32)  9.86 us
    dot_general x4, matrix products, step(): prob_grad = jnp.dot(up_block, values.T, preferred_element_type=jnp.float32)  8.98 us
  transfers between devices with their start and end apart: 6, of which 4 were waited for; matrix products, arithmetic and copies ran while one was open for 26% of the time, Pallas kernels for 0%

commit v1 on v0

v1 whole, which is shorter than its diff:
```python
import functools
import math

import jax
import jax.numpy as jnp
from jax import lax
from jax.experimental import pallas as pl
from jax.experimental.pallas import tpu as pltpu
from jax.sharding import PartitionSpec as P

MESH = pl.DeviceIdType.MESH
F32 = jnp.float32
BF16 = jnp.bfloat16
TOK = 128
VIEWS = 8
COLS = 16
ROWS = 16
D = 1152
HD = 72
NX = 4
NZ = 4
PACK = 224
WIN = 384
Q_SCALE = math.log2(math.e) / math.sqrt(HD)
QB = 256
NQ = 8


def dot(a, b):
    return jnp.dot(a, b, preferred_element_type=F32)


def remote(src, dst, send, recv, device):
    return pltpu.make_async_remote_copy(
        src_ref=src,
        dst_ref=dst,
        send_sem=send,
        recv_sem=recv,
        device_id=device,
        device_id_type=MESH,
    )


def project_kernel(
    tstep,
    cam,
    bias,
    feat,
    w72,
    noise,
    table,
    latp,
    hid,
    gain,
    w_hbm,
    qkv_out,
    norm_out,
    unit_out,
    inv_out,
    halo_send,
    halo_recv,
    ag,
    win,
    pt,
    sendbuf,
    w_sem,
    out_sem,
    hs_sem,
    hr_sem,
    zs_sem,
    zr_sem,
    xs_sem,
    xr_sem,
    own_sem,
):
    me = lax.axis_index("seq")
    z = me // NX
    x = lax.rem(me, NX)

    def at(zz, xx):
        return {"seq": lax.rem(zz + NZ, NZ) * NX + lax.rem(xx + NX, NX)}

    up = {"seq": lax.rem(me + 1, NX * NZ)}
    down = {"seq": lax.rem(me + NX * NZ - 1, NX * NZ)}
    z_up, z_down = at(z + 1, x), at(z - 1, x)
    peers = [up, down, z_up, z_down] + [at(z, x + d) for d in range(1, NX)]
    barrier = pltpu.get_barrier_semaphore()
    for peer in peers:
        pl.semaphore_signal(barrier, inc=1, device_id=peer, device_id_type=MESH)

    w_copies = []
    for t in range(3):
        start = pl.multiple_of(t * D + z * 256, 128)
        copy = pltpu.make_async_copy(
            w_hbm.at[:, pl.ds(start, WIN)], win.at[:, pl.ds(t * WIN, WIN)], w_sem.at[t]
        )
        copy.start()
        w_copies.append(copy)

    f = feat[...].astype(F32)
    act = (f / (1.0 + jnp.exp(-f))).astype(BF16)
    taps = lax.dot_general(w72[...], act, (((1,), (1,)), ((), ())), preferred_element_type=F32)
    lane = lax.rem(lax.broadcasted_iota(jnp.int32, (8, TOK), 1), COLS)
    part = []
    for r in range(3):
        left = pltpu.roll(taps[r * 24 : r * 24 + 8], 1, 1)
        mid = taps[r * 24 + 8 : r * 24 + 16]
        right = pltpu.roll(taps[r * 24 + 16 : r * 24 + 24], TOK - 1, 1)
        part.append(mid + jnp.where(lane == 0, 0.0, left) + jnp.where(lane == COLS - 1, 0.0, right))
    halo_send[0] = part[0]
    halo_send[1] = part[2]
    pl.semaphore_wait(barrier, len(peers))
    halo_up = remote(halo_send.at[0], halo_recv.at[0], hs_sem.at[0], hr_sem.at[0], up)
    halo_down = remote(halo_send.at[1], halo_recv.at[1], hs_sem.at[1], hr_sem.at[1], down)
    halo_up.start()
    halo_down.start()

    node = lax.broadcasted_iota(jnp.int32, (VIEWS, 64), 1)
    view = lax.broadcasted_iota(jnp.int32, (VIEWS, 64), 0)
    picked = jnp.zeros((VIEWS, 64), jnp.int32)
    for v in range(VIEWS):
        picked = jnp.where(view == v, cam[v], picked)
    onehot = jnp.where(node == picked, 1.0, 0.0).astype(BF16)
    embed = dot(onehot, table[...])
    base = hid[...].astype(F32).reshape(VIEWS, COLS, D) + embed[:, None, :]
    base = base.reshape(TOK, D)

    level = jnp.full((8, TOK), tstep[0], jnp.int32).astype(F32) / 1000.0
    cosine = jnp.cos((level + 0.008) / 1.008 * (math.pi / 2.0))
    signal = cosine * cosine
    keep = jnp.sqrt(signal)
    fade = jnp.sqrt(1.0 - signal)

    row = lax.broadcasted_iota(jnp.int32, (8, TOK), 0)
    bias_rows = jnp.zeros((8, TOK), F32)
    for c in range(4):
        bias_rows = jnp.where(row == c, bias[c], bias_rows)
    own = part[1] + bias_rows
    halo_up.wait_recv()
    halo_down.wait_recv()
    own = own + jnp.where(me > 0, halo_recv[0], 0.0)
    own = own + jnp.where(me < NX * NZ - 1, halo_recv[1], 0.0)
    latent = jnp.transpose(own * keep)
    noisy = latent[:, 0:4] + noise[...].astype(F32) * fade[0:1, 0:1]
    inputs = base
    for c in range(4):
        inputs = inputs + noisy[:, c : c + 1] * latp[c : c + 1, :].astype(F32)

    mean = jnp.mean(inputs, -1, keepdims=True)
    centered = inputs - mean
    variance = jnp.mean(centered * centered, -1, keepdims=True)
    inverse = lax.rsqrt(variance + 1e-06)
    unit = centered * inverse
    ag[0] = (unit * gain[...]).astype(BF16)
    send_up = remote(ag.at[0], ag.at[1], zs_sem.at[0], zr_sem.at[0], z_up)
    send_down = remote(ag.at[0], ag.at[3], zs_sem.at[1], zr_sem.at[1], z_down)
    send_up.start()
    send_down.start()
    unit_out[...] = unit
    inv_out[...] = jnp.broadcast_to(inverse, (TOK, 128))

    for copy in w_copies:
        copy.wait()
    half = TOK // 2
    lo, hi = pl.ds(0, half), pl.ds(half, half)
    pass_up = remote(ag.at[1, lo], ag.at[2, lo], zs_sem.at[2], zr_sem.at[2], z_up)
    pass_down = remote(ag.at[3, hi], ag.at[2, hi], zs_sem.at[3], zr_sem.at[3], z_down)

    sends = []
    locals_ = []
    for r in (0, 1, 3, 2):
        if r == 1:
            send_up.wait_recv()
            pass_up.start()
            send_down.wait_recv()
            pass_down.start()
        if r == 2:
            pass_up.wait_recv()
            pass_down.wait_recv()
        keep_out = pltpu.make_async_copy(ag.at[r], norm_out.at[r], out_sem.at[r])
        keep_out.start()
        locals_.append(keep_out)
        for t in range(3):
            block = dot(ag[r], win[:, t * WIN : (t + 1) * WIN])
            if t == 0:
                block = block * Q_SCALE
            pt[t * WIN : (t + 1) * WIN, :] = jnp.transpose(block)
        band = lax.rem(z - r + NZ, NZ) * NX + x
        for d in (1, 3, 2, 0):
            head = lax.rem(x + d, NX)
            rows = []
            for t in range(3):
                first = pl.multiple_of(t * WIN + 32 * z + HD * head, 8)
                rows.append(pt[pl.ds(first, HD), :])
            rows.append(jnp.zeros((PACK - 3 * HD, TOK), F32))
            sendbuf[r, d] = jnp.concatenate(rows, axis=0).astype(BF16)
            if d == 0:
                copy = pltpu.make_async_copy(sendbuf.at[r, 0], qkv_out.at[band], own_sem.at[r])
                locals_.append(copy)
            else:
                copy = remote(
                    sendbuf.at[r, d], qkv_out.at[band], xs_sem.at[r, d], xr_sem.at[r, d], at(z, x + d)
                )
                sends.append(copy)
            copy.start()

    for r in (0, 1, 3, 2):
        for d in range(1, NX):
            band = lax.rem(z - r + NZ, NZ) * NX + lax.rem(x - d + NX, NX)
            remote(
                sendbuf.at[r, d], qkv_out.at[band], xs_sem.at[r, d], xr_sem.at[r, d], at(z, x + d)
            ).wait_recv()
    for copy in sends:
        copy.wait_send()
    for copy in (halo_up, halo_down, send_up, send_down, pass_up, pass_down):
        copy.wait_send()
    for copy in locals_:
        copy.wait()


def attend_kernel(
    groups,
    datas,
    qkv,
    cot,
    unit,
    inv,
    gain,
    norm_hbm,
    w_hbm,
    att,
    hgrad,
    wgrad,
    w_all,
    nall,
    p_all,
    s_ref,
    q_t,
    k_t,
    v_t,
    q_r,
    k_r,
    v_r,
    do_t,
    dos_t,
    dos_r,
    rt,
    dq,
    send_kv,
    send_q,
    recv_kv,
    recv_q,
    g_t,
    g_all,
    gw,
    send_w,
    recv_w,
    w_sem,
    nl_sem,
    ns_sem,
    nr_sem,
    kvs_sem,
    kvr_sem,
    qs_sem,
    qr_sem,
    ws_sem,
    wr_sem,
):
    me = lax.axis_index("seq")
    z = me // NX
    x = lax.rem(me, NX)
    seqs = NX * NZ
    reps = groups * datas
    mine = lax.axis_index("grp") * datas + lax.axis_index("dp")

    def rep_at(i):
        return {"grp": i // datas, "dp": lax.rem(i, datas)}

    barrier = pltpu.get_barrier_semaphore()

    def greet_seq(i, c):
        peer = {"seq": lax.rem(me + i, seqs)}
        pl.semaphore_signal(barrier, inc=1, device_id=peer, device_id_type=MESH)
        return c

    def greet_rep(i, c):
        peer = rep_at(lax.rem(mine + i, reps))
        pl.semaphore_signal(barrier, inc=1, device_id=peer, device_id_type=MESH)
        return c

    lax.fori_loop(1, seqs, greet_seq, 0)
    lax.fori_loop(1, reps, greet_rep, 0)
    w_copy = pltpu.make_async_copy(w_hbm, w_all, w_sem)
    w_copy.start()
    own_norm = pltpu.make_async_copy(norm_hbm, nall.at[0], nl_sem)
    own_norm.start()
    pl.semaphore_wait(barrier, seqs - 1 + reps - 1)

    x_up = {"seq": z * NX + lax.rem(x + 1, NX)}
    x_down = {"seq": z * NX + lax.rem(x + NX - 1, NX)}
    fst, snd = pl.ds(0, 2), pl.ds(2, 2)
    gathers = [
        remote(norm_hbm.at[fst], nall.at[1, fst], ns_sem.at[0], nr_sem.at[0], x_up),
        remote(norm_hbm.at[snd], nall.at[3, snd], ns_sem.at[1], nr_sem.at[1], x_down),
        remote(norm_hbm.at[snd], nall.at[1, snd], ns_sem.at[2], nr_sem.at[2], x_up),
        remote(norm_hbm.at[fst], nall.at[3, fst], ns_sem.at[3], nr_sem.at[3], x_down),
    ]
    relays = [
        remote(nall.at[1, fst], nall.at[2, fst], ns_sem.at[4], nr_sem.at[4], x_up),
        remote(nall.at[3, snd], nall.at[2, snd], ns_sem.at[5], nr_sem.at[5], x_down),
    ]
    for copy in gathers:
        copy.start()

    for j in range(ROWS):
        cols = slice(j * TOK, (j + 1) * TOK)
        block = qkv[j].astype(F32)
        q, k, v = block[0:HD], block[HD : 2 * HD], block[2 * HD : 3 * HD]
        q_t[:, cols] = q.astype(BF16)
        k_t[:, cols] = k.astype(BF16)
        ones = jnp.where(lax.broadcasted_iota(jnp.int32, (8, TOK), 0) == 0, 1.0, 0.0)
        v_t[:, cols] = jnp.concatenate([v, ones], axis=0).astype(BF16)
        q_r[cols, :] = jnp.transpose(q).astype(BF16)
        k_r[cols, :] = jnp.transpose(k).astype(BF16)
        v_r[cols, :] = jnp.transpose(v).astype(BF16)
        do_t[:, cols] = jnp.transpose(cot[:, j].reshape(TOK, HD).astype(F32))
    dq[...] = jnp.zeros(dq.shape, F32)

    def forward(i, c):
        cols = pl.ds(pl.multiple_of(i * QB, QB), QB)
        queries = q_t[:, cols]
        top = None
        for n in range(NQ):
            keys = slice(n * QB, (n + 1) * QB)
            s = dot(k_r[keys, :], queries)
            s_ref[keys, :] = s
            high = jnp.max(s.reshape(QB // 8, 8, QB), axis=0)
            top = high if top is None else jnp.maximum(top, high)
        top = jnp.max(top, axis=0, keepdims=True)
        out = jnp.zeros((HD + 8, QB), F32)
        for n in range(NQ):
            keys = slice(n * QB, (n + 1) * QB)
            p = jnp.exp2(s_ref[keys, :] - top).astype(BF16)
            p_all[i, keys, :] = p
            out = out + dot(v_t[:, keys], p)
        scale = 1.0 / out[HD : HD + 1, :]
        out = out[0:HD] * scale
        upstream = do_t[:, cols]
        rt[i] = jnp.broadcast_to(jnp.sum(upstream * out, axis=0, keepdims=True) * scale, (8, QB))
        upstream = upstream * scale
        dos_t[:, cols] = upstream.astype(BF16)
        dos_r[cols, :] = jnp.transpose(upstream).astype(BF16)
        out = jnp.transpose(out).astype(BF16)
        att[:, pl.ds(2 * i, 1)] = out[0:TOK].reshape(VIEWS, 1, COLS, HD)
        att[:, pl.ds(2 * i + 1, 1)] = out[TOK : 2 * TOK].reshape(VIEWS, 1, COLS, HD)
        return c

    lax.fori_loop(0, NQ, forward, 0)

    def kv_copy(band):
        return remote(
            send_kv.at[band], recv_kv.at[me], kvs_sem.at[band], kvr_sem.at[me], {"seq": band}
        )

    def q_copy(band):
        return remote(send_q.at[band], recv_q.at[me], qs_sem.at[band], qr_sem.at[me], {"seq": band})

    def backward(i, c):
        j = lax.rem(i + me // 2, NQ)
        keys = pl.ds(pl.multiple_of(j * QB, QB), QB)
        values = v_r[keys, :]
        keys_t = k_t[:, keys]
        dk = jnp.zeros((QB, HD), F32)
        dv = jnp.zeros((QB, HD), F32)
        for n in range(NQ):
            cols = slice(n * QB, (n + 1) * QB)
            p = p_all[n, keys, :]
            dp = dot(values, dos_t[:, cols])
            ds = (p.astype(F32) * (dp - rt[n][0:1])).astype(BF16)
            dv = dv + dot(p, dos_r[cols, :])
            dk = dk + dot(ds, q_r[cols, :])
            dq[:, cols] += dot(keys_t, ds)
        dk = jnp.transpose(dk * math.log(2.0))
        dv = jnp.transpose(dv)
        both = jnp.concatenate([dk, dv], axis=0).astype(BF16)
        for b in range(2):
            band = 2 * j + b
            send_kv[band] = both[:, b * TOK : (b + 1) * TOK]

            @pl.when(band != me)
            def _():
                kv_copy(band).start()

        @pl.when(i == 3)
        def _():
            gathers[0].wait_recv()
            relays[0].start()
            gathers[1].wait_recv()
            relays[1].start()

        return c

    lax.fori_loop(0, NQ, backward, 0)

    for j in range(ROWS):
        block = dq[:, j * TOK : (j + 1) * TOK] * (HD**-0.5)
        send_q[j] = jnp.concatenate([block, jnp.zeros((8, TOK), F32)], axis=0).astype(BF16)

    def start_q(i, c):
        q_copy(lax.rem(me + i, seqs)).start()
        return c

    lax.fori_loop(1, seqs, start_q, 0)
    recv_kv[me] = send_kv[me]
    recv_q[me] = send_q[me]

    own_norm.wait()
    gathers[2].wait_recv()
    gathers[3].wait_recv()
    relays[0].wait_recv()
    relays[1].wait_recv()
    for d in range(NX):
        for r in range(NZ):
            band = lax.rem(z - r + NZ, NZ) * NX + lax.rem(x - d + NX, NX)
            cols = slice((d * NZ + r) * TOK, (d * NZ + r + 1) * TOK)
            g_t[0:80, cols] = send_q[band]
            g_t[80:PACK, cols] = send_kv[band]
    for n in range(3):
        lanes = slice(n * WIN, (n + 1) * WIN)
        acc = jnp.zeros((PACK, WIN), F32)
        for d in range(NX):
            acc = acc + dot(
                g_t[:, d * 512 : (d + 1) * 512], nall[d, :, :, lanes].reshape(NZ * TOK, WIN)
            )
        acc = jnp.concatenate([acc[0:HD], acc[80:PACK], jnp.zeros((40, WIN), F32)], axis=0)
        gw[lanes, :] = jnp.transpose(acc)
    for b in range(reps):
        block = gw[b * HD : (b + 1) * HD, :]
        send_w[b] = jnp.concatenate([block, jnp.zeros((8, 256), F32)], axis=0).astype(BF16)

    def w_copy_to(i):
        return remote(send_w.at[i], recv_w.at[mine], ws_sem.at[i], wr_sem.at[mine], rep_at(i))

    def start_w(i, c):
        w_copy_to(lax.rem(mine + i, reps)).start()
        return c

    lax.fori_loop(1, reps, start_w, 0)
    recv_w[mine] = send_w[mine]

    def wait_kv(i, c):
        other = lax.rem(me + i, seqs)
        remote(
            send_kv.at[other], recv_kv.at[other], kvs_sem.at[other], kvr_sem.at[other], {"seq": other}
        ).wait_recv()
        return c

    def wait_q(i, c):
        other = lax.rem(me + i, seqs)
        remote(
            send_q.at[other], recv_q.at[other], qs_sem.at[other], qr_sem.at[other], {"seq": other}
        ).wait_recv()
        return c

    lax.fori_loop(1, seqs, wait_kv, 0)
    for h in range(0, ROWS, 2):
        one, two = recv_kv[h].astype(F32), recv_kv[h + 1].astype(F32)
        pair = jnp.concatenate([one[0:HD], two[0:HD]], axis=0)
        g_all[D + h * HD : D + (h + 2) * HD, :] = pair.astype(BF16)
        pair = jnp.concatenate([one[HD : 2 * HD], two[HD : 2 * HD]], axis=0)
        g_all[2 * D + h * HD : 2 * D + (h + 2) * HD, :] = pair.astype(BF16)
    w_copy.wait()
    normed_grad = dot(w_all[:, D : 3 * D], g_all[D : 3 * D, :])
    lax.fori_loop(1, seqs, wait_q, 0)
    for h in range(0, ROWS, 2):
        one, two = recv_q[h].astype(F32), recv_q[h + 1].astype(F32)
        pair = jnp.concatenate([one[0:HD], two[0:HD]], axis=0)
        g_all[h * HD : (h + 2) * HD, :] = pair.astype(BF16)
    normed_grad = normed_grad + dot(w_all[:, 0:D], g_all[0:D, :])
    scaled = jnp.transpose(normed_grad) * gain[...]
    u = unit[...]
    first = jnp.mean(scaled, -1, keepdims=True)
    second = jnp.mean(scaled * u, -1, keepdims=True)
    hgrad[...] = (inv[:, 0:1] * (scaled - first - u * second)).astype(BF16)

    def wait_w(i, c):
        other = lax.rem(mine + i, reps)
        remote(
            send_w.at[other], recv_w.at[other], ws_sem.at[other], wr_sem.at[other], rep_at(other)
        ).wait_recv()
        return c

    lax.fori_loop(1, reps, wait_w, 0)
    total = recv_w[0].astype(F32)
    for b in range(1, reps):
        total = total + recv_w[b].astype(F32)
    wgrad[...] = total[0:HD, 0 : 3 * HD]

    for copy in gathers + relays:
        copy.wait_send()

    def drain(i, c):
        other = lax.rem(me + i, seqs)
        kv_copy(other).wait_send()
        q_copy(other).wait_send()
        return c

    def drain_w(i, c):
        w_copy_to(lax.rem(mine + i, reps)).wait_send()
        return c

    lax.fori_loop(1, seqs, drain, 0)
    lax.fori_loop(1, reps, drain_w, 0)


VM = pl.BlockSpec(memory_space=pltpu.VMEM)
SM = pl.BlockSpec(memory_space=pltpu.SMEM)
ANY = pl.BlockSpec(memory_space=pl.ANY)
DMA = pltpu.SemaphoreType.DMA


def on_device(
    features,
    conv_weight,
    conv_bias,
    noise,
    timestep,
    camera,
    view_table,
    latent_proj,
    hidden,
    ln_gain,
    qkv_weight,
    cotangent,
):
    groups = lax.axis_size("grp")
    datas = lax.axis_size("dp")
    reps = groups * datas
    w72 = jnp.pad(conv_weight.transpose(0, 1, 3, 2), ((0, 0), (0, 0), (0, 4), (0, 0)))
    gain = ln_gain.reshape(1, D)
    qkv, norm4, unit, inv = pl.pallas_call(
        project_kernel,
        out_shape=(
            jax.ShapeDtypeStruct((ROWS, PACK, TOK), BF16),
            jax.ShapeDtypeStruct((NZ, TOK, D), BF16),
            jax.ShapeDtypeStruct((TOK, D), F32),
            jax.ShapeDtypeStruct((TOK, 128), F32),
        ),
        in_specs=[SM, SM, SM, VM, VM, VM, VM, VM, VM, VM, ANY],
        out_specs=(ANY, ANY, VM, VM),
        scratch_shapes=[
            pltpu.VMEM((2, 8, TOK), F32),
            pltpu.VMEM((2, 8, TOK), F32),
            pltpu.VMEM((NZ, TOK, D), BF16),
            pltpu.VMEM((D, 3 * WIN), BF16),
            pltpu.VMEM((3 * WIN, TOK), F32),
            pltpu.VMEM((NZ, NX, PACK, TOK), BF16),
            DMA((3,)),
            DMA((NZ,)),
            DMA((2,)),
            DMA((2,)),
            DMA((4,)),
            DMA((4,)),
            DMA((NZ, NX)),
            DMA((NZ, NX)),
            DMA((NZ,)),
        ],
        compiler_params=pltpu.CompilerParams(
            collective_id=0, has_side_effects=True, vmem_limit_bytes=40 * 2**20
        ),
        name="project",
    )(
        timestep,
        camera.reshape(VIEWS),
        conv_bias,
        features.reshape(TOK, -1),
        w72.reshape(72, -1),
        noise.reshape(TOK, 4),
        view_table,
        latent_proj,
        hidden.reshape(TOK, D),
        gain,
        qkv_weight,
    )
    att, hgrad, wgrad = pl.pallas_call(
        functools.partial(attend_kernel, groups, datas),
        out_shape=(
            jax.ShapeDtypeStruct((VIEWS, ROWS, COLS, HD), BF16),
            jax.ShapeDtypeStruct((TOK, D), BF16),
            jax.ShapeDtypeStruct((D // reps, 3 * HD), F32),
        ),
        in_specs=[VM, VM, VM, VM, VM, ANY, ANY],
        out_specs=(VM, VM, VM),
        scratch_shapes=[
            pltpu.VMEM((D, 3 * D), BF16),
            pltpu.VMEM((NX, NZ, TOK, D), BF16),
            pltpu.VMEM((NQ, 2048, QB), BF16),
            pltpu.VMEM((2048, QB), F32),
            pltpu.VMEM((HD, 2048), BF16),
            pltpu.VMEM((HD, 2048), BF16),
            pltpu.VMEM((HD + 8, 2048), BF16),
            pltpu.VMEM((2048, HD), BF16),
            pltpu.VMEM((2048, HD), BF16),
            pltpu.VMEM((2048, HD), BF16),
            pltpu.VMEM((HD, 2048), F32),
            pltpu.VMEM((HD, 2048), BF16),
            pltpu.VMEM((2048, HD), BF16),
            pltpu.VMEM((NQ, 8, QB), F32),
            pltpu.VMEM((HD, 2048), F32),
            pltpu.VMEM((ROWS, 2 * HD, TOK), BF16),
            pltpu.VMEM((ROWS, HD + 8, TOK), BF16),
            pltpu.VMEM((ROWS, 2 * HD, TOK), BF16),
            pltpu.VMEM((ROWS, HD + 8, TOK), BF16),
            pltpu.VMEM((PACK, 2048), BF16),
            pltpu.VMEM((3 * D, TOK), BF16),
            pltpu.VMEM((D, 256), F32),
            pltpu.VMEM((reps, HD + 8, 256), BF16),
            pltpu.VMEM((reps, HD + 8, 256), BF16),
            DMA,
            DMA,
            DMA((6,)),
            DMA((6,)),
            DMA((ROWS,)),
            DMA((ROWS,)),
            DMA((ROWS,)),
            DMA((ROWS,)),
            DMA((reps,)),
            DMA((reps,)),
        ],
        compiler_params=pltpu.CompilerParams(
            collective_id=1, has_side_effects=True, vmem_limit_bytes=60 * 2**20
        ),
        name="attend",
    )(qkv, cotangent.reshape(VIEWS, ROWS, COLS, HD), unit, inv, gain, norm4, qkv_weight)
    return (
        att.reshape(cotangent.shape),
        hgrad.reshape(hidden.shape),
        wgrad.reshape(1, D // reps, 3 * HD),
    )


def solution(mesh):
    return jax.shard_map(
        on_device,
        mesh=mesh,
        in_specs=(
            P(("grp", "dp"), None, "seq", None, None),
            P(),
            P(),
            P(("grp", "dp"), None, "seq", None, None),
            P(("grp", "dp")),
            P(("grp", "dp"), None),
            P(),
            P(),
            P(("grp", "dp"), None, "seq", None, None),
            P(),
            P(),
            P(("grp", "dp"), None, None, None, "seq"),
        ),
        out_specs=(
            P(("grp", "dp"), None, None, None, "seq"),
            P(("grp", "dp"), None, "seq", None, None),
            P("seq", ("grp", "dp"), None),
        ),
        check_vma=False,
    )
```

time: 290 us -> 129 us (0.44)
  the two profiles are of different devices: /device:TPU:4 before, /device:TPU:1 now
where the time goes in v1:
time: 129 us; the launch traced here: 128 us
  Pallas kernels  108 us (84%)
  local copies, waits for them, and re-layouts  18.9 us (15%)
  between operations  1.33 us (1%)
    pallas_call x1, Pallas kernels, on_device(): pl.pallas_call(functools.partial(attend_kernel, groups, datas), out_shape...  68.6 us
    pallas_call x1, Pallas kernels, on_device(): pl.pallas_call(project_kernel, out_shape=(jax.ShapeDtypeStruct((ROWS, PAC...  39.3 us
    unnamed x28, local copies, waits for them, and re-layouts  17.4 us

profile of v1, /device:TPU:1, one launch (start us, length us, event | category | flops | bytes accessed | tf_op | source)
XLA Modules:
  0.0 128.0 jit_solution(17788540386364289721)
XLA Ops:
  1.3 0.7 reshape.41.gain
  2.0 0.0 copy-start.8
  2.0 0.8 copy.15
  2.8 0.8 pad.4
  3.6 0.0 copy-start
  3.6 3.3 %copy-done = bf16[1152,3456]{1,0:T(8,128)(2,1)S(1)} copy-done((bf16[1152,3456]{1,0:T(8,128)(2,1)S(1)}, bf16[1152,3456]{1,0:T(8,128)(2,1)}, u32[]{:S(2)}) %copy-start) | copy-done | bytes 7962648
  6.9 0.0 copy-start.4
  6.9 1.0 copy-done.4
  7.8 0.0 copy-start.5
  7.8 0.9 copy-done.5
  8.7 0.0 copy-start.6
  8.7 0.9 copy-done.6
  9.6 0.0 copy-start.9
  9.6 0.7 copy-done.9
  10.3 0.0 copy-start.10
  10.3 0.7 copy-done.10
  11.0 0.0 copy-start.11
  11.0 0.7 copy-done.11
  11.7 39.3 %project.1 = (bf16[16,224,128]{2,1,0:T(8,128)(2,1)S(1)}, bf16[4,128,1152]{2,1,0:T(8,128)(2,1)S(1)}, f32[128,1152]{1,0:T(8,128)S(1)}, f32[128,128]{1,0:T(8,128)S(1)}) custom-call(s32[1]{0:T(128)S(6)} %copy.20.tstep, s32[8]{0:T(128)S(1)} %bitcast.16, f32[4]{0:T(128)S(1)} %copy-done.11, bf16[128,512]{1,0:T(8,128)(2,1)S(1)} %bitcast.14, ...), custom_call_target="tpu_custom_call" | custom-call | tf_op jit(solution)/shard_map/project/pallas_call | solution.py:541
  51.0 0.0 copy-start.1
  51.0 1.0 copy-done.1
  52.0 0.0 copy-start.2
  52.0 0.9 copy-done.2
  52.9 0.0 copy-start.3
  52.9 0.8 copy-done.3
  53.8 0.0 copy-start.7
  53.8 0.6 copy-done.7
  54.4 0.0 copy-done.8
  54.4 68.6 %attend.1 = (bf16[8,16,16,72]{3,2,1,0:T(8,128)(2,1)}, bf16[128,1152]{1,0:T(8,128)(2,1)}, f32[72,216]{1,0:T(8,128)}) custom-call(bf16[16,224,128]{2,1,0:T(8,128)(2,1)} %copy-done.2, bf16[8,16,16,72]{3,2,1,0:T(8,128)(2,1)} %bitcast.18, f32[128,1152]{1,0:T(8,128)} %copy-done.3, f32[128,128]{1,0:T(8,128)} %copy-done.7, f32[1,1152]{1,0:T(1,128)} %copy-done.8, ...), custom_call_target="tpu_custom_call" | custom-call | tf_op jit(solution)/shard_map/attend/pallas_call | solution.py:585
  123.0 1.9 %copy.21 = bf16[1,8,16,16,72]{4,3,2,1,0:T(8,128)(2,1)} copy(bf16[1,8,16,16,72]{4,3,2,1,0:T(8,128)(2,1)} %bitcast.17) | data formatting | bytes 589824
  124.8 1.7 %copy.22 = bf16[1,8,1,16,1152]{4,3,2,1,0:T(8,128)(2,1)} copy(bf16[1,8,1,16,1152]{4,3,2,1,0:T(8,128)(2,1)} %bitcast.19) | data formatting | bytes 589824
  126.5 1.5 %copy.23 = f32[1,72,216]{2,1,0:T(8,128)} copy(f32[1,72,216]{2,1,0:T(8,128)} %bitcast.20) | data formatting | bytes 124416
Async XLA Ops:
  2.0 52.4 %copy-start.8 = (f32[1,1152]{1,0:T(1,128)}, f32[1,1152]{1,0:T(1,128)S(1)}, u32[]{:S(2)}) copy-start(f32[1,1152]{1,0:T(1,128)S(1)} %reshape.41.gain) | copy-start | bytes 13828
  3.6 3.3 %copy-start = (bf16[1152,3456]{1,0:T(8,128)(2,1)S(1)}, bf16[1152,3456]{1,0:T(8,128)(2,1)}, u32[]{:S(2)}) copy-start(bf16[1152,3456]{1,0:T(8,128)(2,1)} %w_hbm.3) | copy-start | bytes 23887876
  6.9 1.0 copy-start.4
  7.8 0.9 copy-start.5
  8.7 0.9 copy-start.6
  9.6 0.7 copy-start.9
  10.3 0.7 copy-start.10
  11.0 0.7 copy-start.11
  51.0 1.0 copy-start.1
  52.0 0.9 copy-start.2
  52.9 0.8 copy-start.3
  53.8 0.6 copy-start.7

commit v2 on v1

v2 whole, which is shorter than its diff:
```python
import functools
import math

import jax
import jax.numpy as jnp
from jax import lax
from jax.experimental import pallas as pl
from jax.experimental.pallas import tpu as pltpu
from jax.sharding import PartitionSpec as P

MESH = pl.DeviceIdType.MESH
F32 = jnp.float32
BF16 = jnp.bfloat16
TOK = 128
VIEWS = 8
COLS = 16
ROWS = 16
D = 1152
HD = 72
NX = 4
NZ = 4
PACK = 224
WIN = 384
SEQS = NX * NZ
Q_SCALE = math.log2(math.e) / math.sqrt(HD)
QB = 256
NQ = 8


def dot(a, b):
    return jnp.dot(a, b, preferred_element_type=F32)


def remote(src, dst, send, recv, device):
    return pltpu.make_async_remote_copy(
        src_ref=src,
        dst_ref=dst,
        send_sem=send,
        recv_sem=recv,
        device_id=device,
        device_id_type=MESH,
    )


def layer_kernel(
    groups,
    datas,
    feat_h,
    w_tap_h,
    bias_h,
    noise_h,
    tstep_h,
    cam_h,
    table_h,
    latp_h,
    hid_h,
    gain_h,
    w_hbm,
    cot_h,
    att_h,
    hgrad_h,
    wgrad_h,
    feat,
    w_tap,
    noise,
    table,
    latp,
    hid,
    gain,
    cot,
    tstep,
    cam,
    bias,
    in_sem,
    halo_send,
    halo_recv,
    unit_s,
    inv_s,
    pt,
    sendbuf,
    qkv,
    w_all,
    nall,
    p_all,
    s_ref,
    q_t,
    k_t,
    v_t,
    q_r,
    k_r,
    v_r,
    do_t,
    dos_t,
    dos_r,
    rt,
    dq,
    send_kv,
    send_q,
    recv_kv,
    recv_q,
    g_t,
    g_all,
    gw,
    send_w,
    recv_w,
    att,
    hgrad,
    wgrad,
    out_sem,
    hs_sem,
    hr_sem,
    zs_sem,
    zr_sem,
    xs_sem,
    xr_sem,
    ns_sem,
    nr_sem,
    kvs_sem,
    kvr_sem,
    qs_sem,
    qr_sem,
    ws_sem,
    wr_sem,
):
    me = lax.axis_index("seq")
    z = me // NX
    x = lax.rem(me, NX)
    reps = groups * datas
    mine = lax.axis_index("grp") * datas + lax.axis_index("dp")

    def at(zz, xx):
        return {"seq": lax.rem(zz + NZ, NZ) * NX + lax.rem(xx + NX, NX)}

    def rep_at(i):
        return {"grp": i // datas, "dp": lax.rem(i, datas)}

    def band_of(d, r):
        return lax.rem(z - r + NZ, NZ) * NX + lax.rem(x - d + NX, NX)

    barrier = pltpu.get_barrier_semaphore()

    def greet_seq(i, c):
        peer = {"seq": lax.rem(me + i, SEQS)}
        pl.semaphore_signal(barrier, inc=1, device_id=peer, device_id_type=MESH)
        return c

    def greet_rep(i, c):
        peer = rep_at(lax.rem(mine + i, reps))
        pl.semaphore_signal(barrier, inc=1, device_id=peer, device_id_type=MESH)
        return c

    fetches = []
    pairs = (
        (feat_h, feat),
        (w_tap_h, w_tap),
        (noise_h, noise),
        (tstep_h, tstep),
        (cam_h, cam),
        (bias_h, bias),
        (table_h, table),
        (latp_h, latp),
        (hid_h, hid),
        (gain_h, gain),
        (w_hbm, w_all),
        (cot_h, cot),
    )
    for n, (src, dst) in enumerate(pairs):
        copy = pltpu.make_async_copy(src, dst, in_sem.at[n])
        copy.start()
        fetches.append(copy)
    lax.fori_loop(1, SEQS, greet_seq, 0)
    lax.fori_loop(1, reps, greet_rep, 0)

    fetches[0].wait()
    fetches[1].wait()
    f = feat[...].astype(F32)
    act = (f / (1.0 + jnp.exp(-f))).astype(BF16)
    lane = lax.rem(lax.broadcasted_iota(jnp.int32, (4, TOK), 1), COLS)
    part = []
    for r in range(3):
        taps = [
            lax.dot_general(
                w_tap[r * 3 + c], act, (((1,), (1,)), ((), ())), preferred_element_type=F32
            )
            for c in range(3)
        ]
        left = jnp.where(lane == 0, 0.0, pltpu.roll(taps[0], 1, 1))
        right = jnp.where(lane == COLS - 1, 0.0, pltpu.roll(taps[2], TOK - 1, 1))
        part.append(taps[1] + left + right)
    halo_send[0, 0:4] = part[0]
    halo_send[1, 0:4] = part[2]
    pl.semaphore_wait(barrier, SEQS - 1 + reps - 1)
    up = {"seq": lax.rem(me + 1, SEQS)}
    down = {"seq": lax.rem(me + SEQS - 1, SEQS)}
    halo_up = remote(halo_send.at[0], halo_recv.at[0], hs_sem.at[0], hr_sem.at[0], up)
    halo_down = remote(halo_send.at[1], halo_recv.at[1], hs_sem.at[1], hr_sem.at[1], down)
    halo_up.start()
    halo_down.start()

    for n in range(2, 10):
        fetches[n].wait()
    node = lax.broadcasted_iota(jnp.int32, (VIEWS, 64), 1)
    view = lax.broadcasted_iota(jnp.int32, (VIEWS, 64), 0)
    picked = jnp.zeros((VIEWS, 64), jnp.int32)
    for v in range(VIEWS):
        picked = jnp.where(view == v, cam[0, v], picked)
    onehot = jnp.where(node == picked, 1.0, 0.0).astype(BF16)
    embed = dot(onehot, table[...])
    base = hid[...].astype(F32).reshape(VIEWS, COLS, D) + embed[:, None, :]
    base = base.reshape(TOK, D)
    level = jnp.full((4, TOK), tstep[0], jnp.int32).astype(F32) / 1000.0
    cosine = jnp.cos((level + 0.008) / 1.008 * (math.pi / 2.0))
    signal = cosine * cosine
    keep = jnp.sqrt(signal)
    fade = jnp.sqrt(1.0 - signal)
    noises = noise[...].astype(F32)
    noises = jnp.concatenate([noises[v] for v in range(VIEWS)], axis=1)
    row = lax.broadcasted_iota(jnp.int32, (4, TOK), 0)
    bias_rows = jnp.zeros((4, TOK), F32)
    for c in range(4):
        bias_rows = jnp.where(row == c, bias[c], bias_rows)
    own = part[1] + bias_rows
    halo_up.wait_recv()
    halo_down.wait_recv()
    own = own + jnp.where(me > 0, halo_recv[0, 0:4], 0.0)
    own = own + jnp.where(me < SEQS - 1, halo_recv[1, 0:4], 0.0)
    noisy = own * keep + noises * fade
    noisy = jnp.transpose(jnp.concatenate([noisy, jnp.zeros((4, TOK), F32)], axis=0))
    inputs = base
    for c in range(4):
        inputs = inputs + noisy[:, c : c + 1] * latp[c : c + 1, :].astype(F32)

    mean = jnp.mean(inputs, -1, keepdims=True)
    centered = inputs - mean
    variance = jnp.mean(centered * centered, -1, keepdims=True)
    inverse = lax.rsqrt(variance + 1e-06)
    unit = centered * inverse
    gains = gain[...].reshape(1, D)
    nall[0, 0] = (unit * gains).astype(BF16)

    half = TOK // 2
    lo, hi = pl.ds(0, half), pl.ds(half, half)
    z_up, z_down = at(z + 1, x), at(z - 1, x)
    x_up, x_down = at(z, x + 1), at(z, x - 1)

    def gather_z(d, n):
        return (
            remote(nall.at[d, 0], nall.at[d, 1], zs_sem.at[n], zr_sem.at[n], z_up),
            remote(nall.at[d, 0], nall.at[d, 3], zs_sem.at[n + 1], zr_sem.at[n + 1], z_down),
            remote(nall.at[d, 1, lo], nall.at[d, 2, lo], zs_sem.at[n + 2], zr_sem.at[n + 2], z_up),
            remote(
                nall.at[d, 3, hi], nall.at[d, 2, hi], zs_sem.at[n + 3], zr_sem.at[n + 3], z_down
            ),
        )

    near = gather_z(0, 0)
    far = gather_z(2, 4)

    def gather_x(r):
        return (
            remote(nall.at[0, r], nall.at[1, r], ns_sem.at[r, 1], nr_sem.at[r, 1], x_up),
            remote(nall.at[0, r], nall.at[3, r], ns_sem.at[r, 3], nr_sem.at[r, 3], x_down),
        )

    side = [gather_x(r) for r in range(NZ)]
    across = remote(nall.at[0, 0], nall.at[2, 0], ns_sem.at[0, 2], nr_sem.at[0, 2], at(z, x + 2))
    near[0].start()
    near[1].start()
    unit_s[...] = unit
    inv_s[...] = jnp.broadcast_to(inverse, (TOK, 128))

    ones = jnp.where(lax.broadcasted_iota(jnp.int32, (8, TOK), 0) == 0, 1.0, 0.0)
    qkv_sends = {}

    def project(r):
        for t in range(3):
            start = pl.multiple_of(t * D + z * 256, 128)
            block = dot(nall[0, r], w_all[:, pl.ds(start, WIN)])
            if t == 0:
                block = block * Q_SCALE
            pt[t * WIN : (t + 1) * WIN, :] = jnp.transpose(block)
        for d in (1, 3, 2, 0):
            head = lax.rem(x + d, NX)
            rows = []
            for t in range(3):
                first = pl.multiple_of(t * WIN + 32 * z + HD * head, 8)
                rows.append(pt[pl.ds(first, HD), :])
            rows.append(jnp.zeros((PACK - 3 * HD, TOK), F32))
            block = jnp.concatenate(rows, axis=0).astype(BF16)
            if d == 0:
                qkv[0, r] = block
            else:
                sendbuf[r, d] = block
                copy = remote(
                    sendbuf.at[r, d], qkv.at[d, r], xs_sem.at[r, d], xr_sem.at[r, d], at(z, x + d)
                )
                copy.start()
                qkv_sends[r, d] = copy

    def spread(r):
        for d in range(NX):
            if d > 0:
                qkv_sends[r, d].wait_recv()
            n = d * NZ + r
            cols = slice(n * TOK, (n + 1) * TOK)
            block = qkv[d, r].astype(F32)
            q, k, v = block[0:HD], block[HD : 2 * HD], block[2 * HD : 3 * HD]
            q_t[:, cols] = q.astype(BF16)
            k_t[:, cols] = k.astype(BF16)
            v_t[:, cols] = jnp.concatenate([v, ones], axis=0).astype(BF16)
            q_r[cols, :] = jnp.transpose(q).astype(BF16)
            k_r[cols, :] = jnp.transpose(k).astype(BF16)
            v_r[cols, :] = jnp.transpose(v).astype(BF16)

    fetches[10].wait()
    project(0)
    side[0][0].start()
    side[0][1].start()
    across.start()
    fetches[11].wait()
    for d in range(NX):
        for r in range(NZ):
            n = d * NZ + r
            block = cot[:, pl.ds(band_of(d, r), 1)].reshape(TOK, HD).astype(F32)
            do_t[:, n * TOK : (n + 1) * TOK] = jnp.transpose(block)
    dq[...] = jnp.zeros(dq.shape, F32)
    spread(0)
    near[0].wait_recv()
    near[2].start()
    near[1].wait_recv()
    near[3].start()
    project(1)
    project(3)
    spread(1)
    spread(3)
    near[2].wait_recv()
    near[3].wait_recv()
    project(2)
    for r in (1, 3, 2):
        side[r][0].start()
        side[r][1].start()
    across.wait_recv()
    far[0].start()
    far[1].start()
    spread(2)

    def forward(i, c):
        cols = pl.ds(pl.multiple_of(i * QB, QB), QB)
        queries = q_t[:, cols]
        top = None
        for n in range(NQ):
            keys = slice(n * QB, (n + 1) * QB)
            s = dot(k_r[keys, :], queries)
            s_ref[keys, :] = s
            high = jnp.max(s.reshape(QB // 8, 8, QB), axis=0)
            top = high if top is None else jnp.maximum(top, high)
        top = jnp.max(top, axis=0, keepdims=True)
        out = jnp.zeros((HD + 8, QB), F32)
        for n in range(NQ):
            keys = slice(n * QB, (n + 1) * QB)
            p = jnp.exp2(s_ref[keys, :] - top).astype(BF16)
            p_all[i, keys, :] = p
            out = out + dot(v_t[:, keys], p)
        scale = 1.0 / out[HD : HD + 1, :]
        out = out[0:HD] * scale
        upstream = do_t[:, cols]
        rt[i] = jnp.broadcast_to(jnp.sum(upstream * out, axis=0, keepdims=True) * scale, (8, QB))
        upstream = upstream * scale
        dos_t[:, cols] = upstream.astype(BF16)
        dos_r[cols, :] = jnp.transpose(upstream).astype(BF16)
        out = jnp.transpose(out).astype(BF16)
        for b in range(2):
            band = band_of(i // 2, lax.rem(i, 2) * 2 + b)
            block = out[b * TOK : (b + 1) * TOK].reshape(VIEWS, 1, COLS, HD)
            att[:, pl.ds(band, 1)] = block
        return c

    lax.fori_loop(0, NQ, forward, 0)
    att_out = pltpu.make_async_copy(att, att_h, out_sem.at[0])
    att_out.start()

    def kv_copy(pos, band):
        return remote(
            send_kv.at[pos], recv_kv.at[me], kvs_sem.at[pos], kvr_sem.at[me], {"seq": band}
        )

    def q_copy(pos, band):
        return remote(send_q.at[pos], recv_q.at[me], qs_sem.at[pos], qr_sem.at[me], {"seq": band})

    def backward(j, c):
        keys = pl.ds(pl.multiple_of(j * QB, QB), QB)
        values = v_r[keys, :]
        keys_t = k_t[:, keys]
        dk = jnp.zeros((QB, HD), F32)
        dv = jnp.zeros((QB, HD), F32)
        for n in range(NQ):
            cols = slice(n * QB, (n + 1) * QB)
            p = p_all[n, keys, :]
            dp = dot(values, dos_t[:, cols])
            ds = (p.astype(F32) * (dp - rt[n][0:1])).astype(BF16)
            dv = dv + dot(p, dos_r[cols, :])
            dk = dk + dot(ds, q_r[cols, :])
            dq[:, cols] += dot(keys_t, ds)
        dk = jnp.transpose(dk * math.log(2.0))
        dv = jnp.transpose(dv)
        both = jnp.concatenate([dk, dv], axis=0).astype(BF16)
        for b in range(2):
            pos = 2 * j + b
            send_kv[pos] = both[:, b * TOK : (b + 1) * TOK]

            @pl.when(pos > 0)
            def _():
                kv_copy(pos, band_of(pos // NZ, lax.rem(pos, NZ))).start()

        @pl.when(j == 3)
        def _():
            far[0].wait_recv()
            far[2].start()
            far[1].wait_recv()
            far[3].start()

        return c

    lax.fori_loop(0, NQ, backward, 0)

    for pos in range(SEQS):
        block = dq[:, pos * TOK : (pos + 1) * TOK] * (HD**-0.5)
        send_q[pos] = jnp.concatenate([block, jnp.zeros((8, TOK), F32)], axis=0).astype(BF16)
        if pos > 0:
            q_copy(pos, band_of(pos // NZ, pos % NZ)).start()
    recv_kv[me] = send_kv[0]
    recv_q[me] = send_q[0]

    for pos in range(SEQS):
        cols = slice(pos * TOK, (pos + 1) * TOK)
        g_t[0:80, cols] = send_q[pos]
        g_t[80:PACK, cols] = send_kv[pos]
    for r in (1, 3, 2):
        side[r][0].wait_recv()
        side[r][1].wait_recv()
    side[0][0].wait_recv()
    side[0][1].wait_recv()
    far[2].wait_recv()
    far[3].wait_recv()
    for n in range(3):
        lanes = slice(n * WIN, (n + 1) * WIN)
        acc = jnp.zeros((PACK, WIN), F32)
        for d in range(NX):
            acc = acc + dot(
                g_t[:, d * 512 : (d + 1) * 512], nall[d, :, :, lanes].reshape(NZ * TOK, WIN)
            )
        acc = jnp.concatenate([acc[0:HD], acc[80:PACK], jnp.zeros((40, WIN), F32)], axis=0)
        gw[lanes, :] = jnp.transpose(acc)
    for b in range(reps):
        block = gw[b * HD : (b + 1) * HD, :]
        send_w[b] = jnp.concatenate([block, jnp.zeros((8, 256), F32)], axis=0).astype(BF16)

    def w_copy_to(i):
        return remote(send_w.at[i], recv_w.at[mine], ws_sem.at[i], wr_sem.at[mine], rep_at(i))

    def start_w(i, c):
        w_copy_to(lax.rem(mine + i, reps)).start()
        return c

    lax.fori_loop(1, reps, start_w, 0)
    recv_w[mine] = send_w[mine]

    def wait_kv(i, c):
        other = lax.rem(me + i, SEQS)
        remote(
            send_kv.at[0], recv_kv.at[other], kvs_sem.at[0], kvr_sem.at[other], {"seq": other}
        ).wait_recv()
        return c

    def wait_q(i, c):
        other = lax.rem(me + i, SEQS)
        remote(
            send_q.at[0], recv_q.at[other], qs_sem.at[0], qr_sem.at[other], {"seq": other}
        ).wait_recv()
        return c

    lax.fori_loop(1, SEQS, wait_kv, 0)
    for h in range(0, SEQS, 2):
        one, two = recv_kv[h].astype(F32), recv_kv[h + 1].astype(F32)
        pair = jnp.concatenate([one[0:HD], two[0:HD]], axis=0)
        g_all[D + h * HD : D + (h + 2) * HD, :] = pair.astype(BF16)
        pair = jnp.concatenate([one[HD : 2 * HD], two[HD : 2 * HD]], axis=0)
        g_all[2 * D + h * HD : 2 * D + (h + 2) * HD, :] = pair.astype(BF16)
    normed_grad = dot(w_all[:, D : 3 * D], g_all[D : 3 * D, :])
    lax.fori_loop(1, SEQS, wait_q, 0)
    for h in range(0, SEQS, 2):
        one, two = recv_q[h].astype(F32), recv_q[h + 1].astype(F32)
        pair = jnp.concatenate([one[0:HD], two[0:HD]], axis=0)
        g_all[h * HD : (h + 2) * HD, :] = pair.astype(BF16)
    normed_grad = normed_grad + dot(w_all[:, 0:D], g_all[0:D, :])
    scaled = jnp.transpose(normed_grad) * gain[...].reshape(1, D)
    u = unit_s[...]
    first = jnp.mean(scaled, -1, keepdims=True)
    second = jnp.mean(scaled * u, -1, keepdims=True)
    hgrad[...] = (inv_s[:, 0:1] * (scaled - first - u * second)).astype(BF16)
    hgrad_out = pltpu.make_async_copy(hgrad, hgrad_h, out_sem.at[1])
    hgrad_out.start()

    def wait_w(i, c):
        other = lax.rem(mine + i, reps)
        remote(
            send_w.at[0], recv_w.at[other], ws_sem.at[0], wr_sem.at[other], rep_at(other)
        ).wait_recv()
        return c

    lax.fori_loop(1, reps, wait_w, 0)
    total = recv_w[0].astype(F32)
    for b in range(1, reps):
        total = total + recv_w[b].astype(F32)
    wgrad[...] = total[0:HD, 0 : 3 * HD]
    wgrad_out = pltpu.make_async_copy(wgrad, wgrad_h, out_sem.at[2])
    wgrad_out.start()

    for copy in (halo_up, halo_down, across) + near + far:
        copy.wait_send()
    for pair in side:
        pair[0].wait_send()
        pair[1].wait_send()
    for copy in qkv_sends.values():
        copy.wait_send()

    def drain(i, c):
        kv_copy(i, lax.rem(me + i, SEQS)).wait_send()
        q_copy(i, lax.rem(me + i, SEQS)).wait_send()
        return c

    def drain_w(i, c):
        w_copy_to(lax.rem(mine + i, reps)).wait_send()
        return c

    lax.fori_loop(1, SEQS, drain, 0)
    lax.fori_loop(1, reps, drain_w, 0)
    att_out.wait()
    hgrad_out.wait()
    wgrad_out.wait()


def hand_out(*refs):
    count = len(refs) // 2
    sem = refs[-1]
    copies = [
        pltpu.make_async_copy(refs[n], refs[count + n], sem.at[n]) for n in range(count)
    ]
    for copy in copies:
        copy.start()
    for copy in copies:
        copy.wait()


ANY = pl.BlockSpec(memory_space=pl.ANY)
DMA = pltpu.SemaphoreType.DMA


def on_device(
    features,
    conv_weight,
    conv_bias,
    noise,
    timestep,
    camera,
    view_table,
    latent_proj,
    hidden,
    ln_gain,
    qkv_weight,
    cotangent,
):
    groups = lax.axis_size("grp")
    datas = lax.axis_size("dp")
    reps = groups * datas
    depth = features.shape[-1]
    outs = (
        jax.ShapeDtypeStruct((VIEWS, ROWS, COLS, HD), BF16),
        jax.ShapeDtypeStruct((TOK, D), BF16),
        jax.ShapeDtypeStruct((D // reps, 3 * HD), F32),
    )
    results = pl.pallas_call(
        functools.partial(layer_kernel, groups, datas),
        out_shape=outs,
        in_specs=[ANY] * 12,
        out_specs=(ANY,) * 3,
        scratch_shapes=[
            pltpu.VMEM((TOK, depth), BF16),
            pltpu.VMEM((9, 4, depth), BF16),
            pltpu.VMEM((VIEWS, 4, COLS), BF16),
            pltpu.VMEM(view_table.shape, BF16),
            pltpu.VMEM(latent_proj.shape, BF16),
            pltpu.VMEM((TOK, D), BF16),
            pltpu.VMEM((D,), F32),
            pltpu.VMEM((VIEWS, ROWS, COLS, HD), BF16),
            pltpu.SMEM((1,), jnp.int32),
            pltpu.SMEM((1, VIEWS), jnp.int32),
            pltpu.SMEM((4,), F32),
            DMA((12,)),
            pltpu.VMEM((2, 8, TOK), F32),
            pltpu.VMEM((2, 8, TOK), F32),
            pltpu.VMEM((TOK, D), F32),
            pltpu.VMEM((TOK, 128), F32),
            pltpu.VMEM((3 * WIN, TOK), F32),
            pltpu.VMEM((NZ, NX, PACK, TOK), BF16),
            pltpu.VMEM((NX, NZ, PACK, TOK), BF16),
            pltpu.VMEM((D, 3 * D), BF16),
            pltpu.VMEM((NX, NZ, TOK, D), BF16),
            pltpu.VMEM((NQ, 2048, QB), BF16),
            pltpu.VMEM((2048, QB), F32),
            pltpu.VMEM((HD, 2048), BF16),
            pltpu.VMEM((HD, 2048), BF16),
            pltpu.VMEM((HD + 8, 2048), BF16),
            pltpu.VMEM((2048, HD), BF16),
            pltpu.VMEM((2048, HD), BF16),
            pltpu.VMEM((2048, HD), BF16),
            pltpu.VMEM((HD, 2048), F32),
            pltpu.VMEM((HD, 2048), BF16),
            pltpu.VMEM((2048, HD), BF16),
            pltpu.VMEM((NQ, 8, QB), F32),
            pltpu.VMEM((HD, 2048), F32),
            pltpu.VMEM((SEQS, 2 * HD, TOK), BF16),
            pltpu.VMEM((SEQS, HD + 8, TOK), BF16),
            pltpu.VMEM((SEQS, 2 * HD, TOK), BF16),
            pltpu.VMEM((SEQS, HD + 8, TOK), BF16),
            pltpu.VMEM((PACK, 2048), BF16),
            pltpu.VMEM((3 * D, TOK), BF16),
            pltpu.VMEM((D, 256), F32),
            pltpu.VMEM((reps, HD + 8, 256), BF16),
            pltpu.VMEM((reps, HD + 8, 256), BF16),
            pltpu.VMEM((VIEWS, ROWS, COLS, HD), BF16),
            pltpu.VMEM((TOK, D), BF16),
            pltpu.VMEM((D // reps, 3 * HD), F32),
            DMA((3,)),
            DMA((2,)),
            DMA((2,)),
            DMA((8,)),
            DMA((8,)),
            DMA((NZ, NX)),
            DMA((NZ, NX)),
            DMA((NZ, NX)),
            DMA((NZ, NX)),
            DMA((SEQS,)),
            DMA((SEQS,)),
            DMA((SEQS,)),
            DMA((SEQS,)),
            DMA((reps,)),
            DMA((reps,)),
        ],
        compiler_params=pltpu.CompilerParams(
            collective_id=0, has_side_effects=True, vmem_limit_bytes=62 * 2**20
        ),
        name="layer",
    )(
        features.reshape(TOK, depth),
        conv_weight.transpose(0, 1, 3, 2).reshape(9, 4, depth),
        conv_bias,
        noise.transpose(0, 1, 2, 4, 3).reshape(VIEWS, 4, COLS),
        timestep,
        camera,
        view_table,
        latent_proj,
        hidden.reshape(TOK, D),
        ln_gain,
        qkv_weight,
        cotangent.reshape(VIEWS, ROWS, COLS, HD),
    )
    att, hgrad, wgrad = pl.pallas_call(
        hand_out,
        out_shape=outs,
        in_specs=[ANY] * 3,
        out_specs=(ANY,) * 3,
        scratch_shapes=[DMA((3,))],
        name="hand_out",
    )(*results)
    return (
        att.reshape(cotangent.shape),
        hgrad.reshape(hidden.shape),
        wgrad.reshape(1, D // reps, 3 * HD),
    )


def solution(mesh):
    return jax.shard_map(
        on_device,
        mesh=mesh,
        in_specs=(
            P(("grp", "dp"), None, "seq", None, None),
            P(),
            P(),
            P(("grp", "dp"), None, "seq", None, None),
            P(("grp", "dp")),
            P(("grp", "dp"), None),
            P(),
            P(),
            P(("grp", "dp"), None, "seq", None, None),
            P(),
            P(),
            P(("grp", "dp"), None, None, None, "seq"),
        ),
        out_specs=(
            P(("grp", "dp"), None, None, None, "seq"),
            P(("grp", "dp"), None, "seq", None, None),
            P("seq", ("grp", "dp"), None),
        ),
        check_vma=False,
    )
```

time: 129 us -> 125 us (0.969)
  the two profiles are of different devices: /device:TPU:1 before, /device:TPU:57 now
where the time goes in v2:
time: 125 us
  Pallas kernels  123 us (98%)
  between operations  1.45 us (1%)
    pallas_call x1, Pallas kernels, on_device(): pl.pallas_call(functools.partial(layer_kernel, groups, datas), out_shape=...  95 us
    pallas_call x1, Pallas kernels, on_device(): pl.pallas_call(hand_out, out_shape=outs, in_specs=[ANY] * 3, out_specs=(A...  28.2 us

profile of v2, /device:TPU:57, one launch (start us, length us, event | category | flops | bytes accessed | tf_op | source)
XLA Modules:
  0.0 124.7 jit_solution(12730625437664654403)
XLA Ops:
  1.3 95.0 %layer.1 = (bf16[8,16,16,72]{3,2,1,0:T(8,128)(2,1)}, bf16[128,1152]{1,0:T(8,128)(2,1)}, f32[72,216]{1,0:T(8,128)}) custom-call(bf16[128,512]{1,0:T(8,128)(2,1)} %bitcast.18, bf16[9,4,512]{2,1,0:T(4,128)(2,1)} %bitcast.19, f32[4]{0:T(128)} %bias_h.1, bf16[8,4,16]{2,1,0:T(4,128)(2,1)} %bitcast.20, s32[1]{0:T(128)S(6)} %copy.17.tstep_h, s32[1,8]{1,0:T(1,128)} %cam_h.1, ...), custom_call_target="tpu_custom_call" | custom-call | tf_op jit(solution)/shard_map/layer/pallas_call | solution.py:582
  96.3 28.2 %hand_out.1 = (bf16[8,16,16,72]{3,2,1,0:T(8,128)(2,1)}, bf16[128,1152]{1,0:T(8,128)(2,1)}, f32[72,216]{1,0:T(8,128)}) custom-call(bf16[8,16,16,72]{3,2,1,0:T(8,128)(2,1)} %get-tuple-element.9.refs_0_, bf16[128,1152]{1,0:T(8,128)(2,1)} %get-tuple-element.10.refs_1_, f32[72,216]{1,0:T(8,128)} %get-tuple-element.11.refs_2_), custom_call_target="tpu_custom_call" | custom-call | tf_op jit(solution)/shard_map/hand_out/pallas_call | solution.py:668

commit v3 on v2

--- a/solution.py
+++ b/solution.py
@@ -25,6 +25,8 @@
 Q_SCALE = math.log2(math.e) / math.sqrt(HD)
 QB = 256
 NQ = 8
+GROUP = 512
+ORDER = (0, 1, 3, 2)
 
 
 def dot(a, b):
@@ -82,7 +84,8 @@
     w_all,
     nall,
     p_all,
-    s_ref,
+    s_all,
+    tops,
     q_t,
     k_t,
     v_t,
@@ -94,6 +97,7 @@
     dos_r,
     rt,
     dq,
+    ds_s,
     send_kv,
     send_q,
     recv_kv,
@@ -101,6 +105,8 @@
     g_t,
     g_all,
     gw,
+    send_p,
+    recv_p,
     send_w,
     recv_w,
     att,
@@ -115,24 +121,31 @@
     xr_sem,
     ns_sem,
     nr_sem,
+    rs_sem,
+    rr_sem,
     kvs_sem,
     kvr_sem,
     qs_sem,
     qr_sem,
+    ps_sem,
+    pr_sem,
     ws_sem,
     wr_sem,
 ):
     me = lax.axis_index("seq")
     z = me // NX
     x = lax.rem(me, NX)
-    reps = groups * datas
-    mine = lax.axis_index("grp") * datas + lax.axis_index("dp")
+    chips = groups * datas // 2
+    dp = lax.axis_index("dp")
+    core = lax.rem(dp, 2)
+    chip = lax.axis_index("grp") * (datas // 2) + dp // 2
+    partner = {"dp": dp + 1 - 2 * core}
 
     def at(zz, xx):
         return {"seq": lax.rem(zz + NZ, NZ) * NX + lax.rem(xx + NX, NX)}
 
-    def rep_at(i):
-        return {"grp": i // datas, "dp": lax.rem(i, datas)}
+    def chip_at(k):
+        return {"grp": k // (datas // 2), "dp": lax.rem(k, datas // 2) * 2 + core}
 
     def band_of(d, r):
         return lax.rem(z - r + NZ, NZ) * NX + lax.rem(x - d + NX, NX)
@@ -144,8 +157,8 @@
         pl.semaphore_signal(barrier, inc=1, device_id=peer, device_id_type=MESH)
         return c
 
-    def greet_rep(i, c):
-        peer = rep_at(lax.rem(mine + i, reps))
+    def greet_chip(i, c):
+        peer = chip_at(lax.rem(chip + i, chips))
         pl.semaphore_signal(barrier, inc=1, device_id=peer, device_id_type=MESH)
         return c
 
@@ -169,7 +182,8 @@
         copy.start()
         fetches.append(copy)
     lax.fori_loop(1, SEQS, greet_seq, 0)
-    lax.fori_loop(1, reps, greet_rep, 0)
+    lax.fori_loop(1, chips, greet_chip, 0)
+    pl.semaphore_signal(barrier, inc=1, device_id=partner, device_id_type=MESH)
 
     fetches[0].wait()
     fetches[1].wait()
@@ -189,7 +203,7 @@
         part.append(taps[1] + left + right)
     halo_send[0, 0:4] = part[0]
     halo_send[1, 0:4] = part[2]
-    pl.semaphore_wait(barrier, SEQS - 1 + reps - 1)
+    pl.semaphore_wait(barrier, SEQS - 1 + chips)
     up = {"seq": lax.rem(me + 1, SEQS)}
     down = {"seq": lax.rem(me + SEQS - 1, SEQS)}
     halo_up = remote(halo_send.at[0], halo_recv.at[0], hs_sem.at[0], hr_sem.at[0], up)
@@ -241,45 +255,63 @@
     half = TOK // 2
     lo, hi = pl.ds(0, half), pl.ds(half, half)
     z_up, z_down = at(z + 1, x), at(z - 1, x)
-    x_up, x_down = at(z, x + 1), at(z, x - 1)
-
-    def gather_z(d, n):
-        return (
-            remote(nall.at[d, 0], nall.at[d, 1], zs_sem.at[n], zr_sem.at[n], z_up),
-            remote(nall.at[d, 0], nall.at[d, 3], zs_sem.at[n + 1], zr_sem.at[n + 1], z_down),
-            remote(nall.at[d, 1, lo], nall.at[d, 2, lo], zs_sem.at[n + 2], zr_sem.at[n + 2], z_up),
-            remote(
-                nall.at[d, 3, hi], nall.at[d, 2, hi], zs_sem.at[n + 3], zr_sem.at[n + 3], z_down
-            ),
+    x_up, x_down, x_far = at(z, x + 1), at(z, x - 1), at(z, x + 2)
+
+    def by_z(src, dst, n, device):
+        return remote(src, dst, zs_sem.at[n], zr_sem.at[n], device)
+
+    up_lo = by_z(nall.at[0, 0, lo], nall.at[1, 0, lo], 0, z_up)
+    up_hi = by_z(nall.at[0, 0, hi], nall.at[1, 0, hi], 1, z_up)
+    down_hi = by_z(nall.at[0, 0, hi], nall.at[2, 0, hi], 2, z_down)
+    down_lo = by_z(nall.at[0, 0, lo], nall.at[2, 0, lo], 3, z_down)
+    pass_lo = by_z(nall.at[1, 0, lo], nall.at[3, 0, lo], 4, z_up)
+    pass_hi = by_z(nall.at[2, 0, hi], nall.at[3, 0, hi], 5, z_down)
+    far_up = by_z(nall.at[0, 2], nall.at[1, 2], 6, z_up)
+    far_down = by_z(nall.at[0, 2], nall.at[2, 2], 7, z_down)
+
+    def by_x(n, d, device):
+        return remote(nall.at[n, 0], nall.at[n, d], ns_sem.at[n, d], nr_sem.at[n, d], device)
+
+    side = [(by_x(n, 1, x_up), by_x(n, 3, x_down)) for n in range(NZ)]
+    relays = []
+    for n in (0, 3):
+        relay = n // 3 * 2
+        relays.append(
+            (
+                remote(
+                    nall.at[n, 1, lo], nall.at[n, 2, lo], rs_sem.at[relay], rr_sem.at[relay], x_up
+                ),
+                remote(
+                    nall.at[n, 3, hi],
+                    nall.at[n, 2, hi],
+                    rs_sem.at[relay + 1],
+                    rr_sem.at[relay + 1],
+                    x_down,
+                ),
+            )
         )
 
-    near = gather_z(0, 0)
-    far = gather_z(2, 4)
-
-    def gather_x(r):
-        return (
-            remote(nall.at[0, r], nall.at[1, r], ns_sem.at[r, 1], nr_sem.at[r, 1], x_up),
-            remote(nall.at[0, r], nall.at[3, r], ns_sem.at[r, 3], nr_sem.at[r, 3], x_down),
-        )
-
-    side = [gather_x(r) for r in range(NZ)]
-    across = remote(nall.at[0, 0], nall.at[2, 0], ns_sem.at[0, 2], nr_sem.at[0, 2], at(z, x + 2))
-    near[0].start()
-    near[1].start()
+    def relay_x(n):
+        for k in range(2):
+            side[n * 3][k].wait_recv()
+            relays[n][k].start()
+
+    for copy in (up_lo, down_hi, up_hi, down_lo):
+        copy.start()
     unit_s[...] = unit
     inv_s[...] = jnp.broadcast_to(inverse, (TOK, 128))
 
     ones = jnp.where(lax.broadcasted_iota(jnp.int32, (8, TOK), 0) == 0, 1.0, 0.0)
     qkv_sends = {}
 
-    def project(r):
+    def project(n):
         for t in range(3):
             start = pl.multiple_of(t * D + z * 256, 128)
-            block = dot(nall[0, r], w_all[:, pl.ds(start, WIN)])
+            block = dot(nall[n, 0], w_all[:, pl.ds(start, WIN)])
             if t == 0:
                 block = block * Q_SCALE
             pt[t * WIN : (t + 1) * WIN, :] = jnp.transpose(block)
-        for d in (1, 3, 2, 0):
+        for d in (2, 1, 3, 0):
             head = lax.rem(x + d, NX)
             rows = []
             for t in range(3):
@@ -288,22 +320,22 @@
             rows.append(jnp.zeros((PACK - 3 * HD, TOK), F32))
             block = jnp.concatenate(rows, axis=0).astype(BF16)
             if d == 0:
-                qkv[0, r] = block
+                qkv[n, 0] = block
             else:
-                sendbuf[r, d] = block
+                sendbuf[n, d] = block
                 copy = remote(
-                    sendbuf.at[r, d], qkv.at[d, r], xs_sem.at[r, d], xr_sem.at[r, d], at(z, x + d)
+                    sendbuf.at[n, d], qkv.at[n, d], xs_sem.at[n, d], xr_sem.at[n, d], at(z, x + d)
                 )
                 copy.start()
-                qkv_sends[r, d] = copy
-
-    def spread(r):
+                qkv_sends[n, d] = copy
+
+    def spread(n):
         for d in range(NX):
             if d > 0:
-                qkv_sends[r, d].wait_recv()
-            n = d * NZ + r
-            cols = slice(n * TOK, (n + 1) * TOK)
-            block = qkv[d, r].astype(F32)
+                qkv_sends[n, d].wait_recv()
+            pos = n * NX + d
+            cols = slice(pos * TOK, (pos + 1) * TOK)
+            block = qkv[n, d].astype(F32)
             q, k, v = block[0:HD], block[HD : 2 * HD], block[2 * HD : 3 * HD]
             q_t[:, cols] = q.astype(BF16)
             k_t[:, cols] = k.astype(BF16)
@@ -312,70 +344,82 @@
             k_r[cols, :] = jnp.transpose(k).astype(BF16)
             v_r[cols, :] = jnp.transpose(v).astype(BF16)
 
+    def score(group, first, last):
+        cols = slice(group * GROUP, (group + 1) * GROUP)
+        queries = q_t[:, cols]
+        top = None
+        for n in range(first, last):
+            keys = slice(n * QB, (n + 1) * QB)
+            s = dot(k_r[keys, :], queries)
+            s_all[keys, cols] = s
+            high = jnp.max(s.reshape(QB // 8, 8, GROUP), axis=0)
+            top = high if top is None else jnp.maximum(top, high)
+        return top
+
     fetches[10].wait()
     project(0)
-    side[0][0].start()
-    side[0][1].start()
-    across.start()
+    for copy in side[0]:
+        copy.start()
     fetches[11].wait()
-    for d in range(NX):
-        for r in range(NZ):
-            n = d * NZ + r
-            block = cot[:, pl.ds(band_of(d, r), 1)].reshape(TOK, HD).astype(F32)
-            do_t[:, n * TOK : (n + 1) * TOK] = jnp.transpose(block)
+    for n in range(NZ):
+        for d in range(NX):
+            pos = n * NX + d
+            block = cot[:, pl.ds(band_of(d, ORDER[n]), 1)].reshape(TOK, HD).astype(F32)
+            do_t[:, pos * TOK : (pos + 1) * TOK] = jnp.transpose(block)
     dq[...] = jnp.zeros(dq.shape, F32)
+    up_lo.wait_recv()
+    pass_lo.start()
+    down_hi.wait_recv()
+    pass_hi.start()
     spread(0)
-    near[0].wait_recv()
-    near[2].start()
-    near[1].wait_recv()
-    near[3].start()
+    relay_x(0)
+    up_hi.wait_recv()
     project(1)
+    down_lo.wait_recv()
+    project(2)
+    side[1][0].start()
+    side[1][1].start()
+    spread(1)
+    spread(2)
+    pass_lo.wait_recv()
+    pass_hi.wait_recv()
     project(3)
-    spread(1)
+    for n in (3, 2):
+        side[n][0].start()
+        side[n][1].start()
+    for copy in relays[0]:
+        copy.wait_recv()
+    far_up.start()
+    far_down.start()
+
+    for group in range(NZ - 1):
+        tops[group] = score(group, 0, 6)
     spread(3)
-    near[2].wait_recv()
-    near[3].wait_recv()
-    project(2)
-    for r in (1, 3, 2):
-        side[r][0].start()
-        side[r][1].start()
-    across.wait_recv()
-    far[0].start()
-    far[1].start()
-    spread(2)
-
-    def forward(i, c):
-        cols = pl.ds(pl.multiple_of(i * QB, QB), QB)
-        queries = q_t[:, cols]
-        top = None
+    for group in range(NZ - 1):
+        tops[group] = jnp.maximum(tops[group], score(group, 6, NQ))
+    tops[3] = score(3, 0, NQ)
+    for group in range(NZ):
+        cols = slice(group * GROUP, (group + 1) * GROUP)
+        top = jnp.max(tops[group], axis=0, keepdims=True)
+        out = None
         for n in range(NQ):
             keys = slice(n * QB, (n + 1) * QB)
-            s = dot(k_r[keys, :], queries)
-            s_ref[keys, :] = s
-            high = jnp.max(s.reshape(QB // 8, 8, QB), axis=0)
-            top = high if top is None else jnp.maximum(top, high)
-        top = jnp.max(top, axis=0, keepdims=True)
-        out = jnp.zeros((HD + 8, QB), F32)
-        for n in range(NQ):
-            keys = slice(n * QB, (n + 1) * QB)
-            p = jnp.exp2(s_ref[keys, :] - top).astype(BF16)
-            p_all[i, keys, :] = p
-            out = out + dot(v_t[:, keys], p)
+            p = jnp.exp2(s_all[keys, cols] - top).astype(BF16)
+            p_all[keys, cols] = p
+            term = dot(v_t[:, keys], p)
+            out = term if out is None else out + term
         scale = 1.0 / out[HD : HD + 1, :]
         out = out[0:HD] * scale
         upstream = do_t[:, cols]
-        rt[i] = jnp.broadcast_to(jnp.sum(upstream * out, axis=0, keepdims=True) * scale, (8, QB))
+        total = jnp.sum(upstream * out, axis=0, keepdims=True) * scale
+        rt[:, cols] = jnp.broadcast_to(total, (8, GROUP))
         upstream = upstream * scale
         dos_t[:, cols] = upstream.astype(BF16)
         dos_r[cols, :] = jnp.transpose(upstream).astype(BF16)
         out = jnp.transpose(out).astype(BF16)
-        for b in range(2):
-            band = band_of(i // 2, lax.rem(i, 2) * 2 + b)
-            block = out[b * TOK : (b + 1) * TOK].reshape(VIEWS, 1, COLS, HD)
-            att[:, pl.ds(band, 1)] = block
-        return c
-
-    lax.fori_loop(0, NQ, forward, 0)
+        for d in range(NX):
+            block = out[d * TOK : (d + 1) * TOK].reshape(VIEWS, 1, COLS, HD)
+            att[:, pl.ds(band_of(d, ORDER[group]), 1)] = block
     att_out = pltpu.make_async_copy(att, att_h, out_sem.at[0])
     att_out.start()
 
@@ -387,83 +431,81 @@
     def q_copy(pos, band):
         return remote(send_q.at[pos], recv_q.at[me], qs_sem.at[pos], qr_sem.at[me], {"seq": band})
 
-    def backward(j, c):
-        keys = pl.ds(pl.multiple_of(j * QB, QB), QB)
+    def score_grad(keys):
         values = v_r[keys, :]
-        keys_t = k_t[:, keys]
-        dk = jnp.zeros((QB, HD), F32)
-        dv = jnp.zeros((QB, HD), F32)
         for n in range(NQ):
             cols = slice(n * QB, (n + 1) * QB)
-            p = p_all[n, keys, :]
             dp = dot(values, dos_t[:, cols])
-            ds = (p.astype(F32) * (dp - rt[n][0:1])).astype(BF16)
-            dv = dv + dot(p, dos_r[cols, :])
-            dk = dk + dot(ds, q_r[cols, :])
-            dq[:, cols] += dot(keys_t, ds)
+            p = p_all[keys, cols].astype(F32)
+            ds_s[:, cols] = (p * (dp - rt[0:1, cols])).astype(BF16)
+
+    def key_grads(keys):
+        dv = dot(p_all[keys, :], dos_r[...])
+        dk = dot(ds_s[...], q_r[...])
         dk = jnp.transpose(dk * math.log(2.0))
         dv = jnp.transpose(dv)
         both = jnp.concatenate([dk, dv], axis=0).astype(BF16)
-        for b in range(2):
-            pos = 2 * j + b
-            send_kv[pos] = both[:, b * TOK : (b + 1) * TOK]
-
-            @pl.when(pos > 0)
-            def _():
-                kv_copy(pos, band_of(pos // NZ, lax.rem(pos, NZ))).start()
-
-        @pl.when(j == 3)
-        def _():
-            far[0].wait_recv()
-            far[2].start()
-            far[1].wait_recv()
-            far[3].start()
-
-        return c
-
-    lax.fori_loop(0, NQ, backward, 0)
-
-    for pos in range(SEQS):
-        block = dq[:, pos * TOK : (pos + 1) * TOK] * (HD**-0.5)
-        send_q[pos] = jnp.concatenate([block, jnp.zeros((8, TOK), F32)], axis=0).astype(BF16)
-        if pos > 0:
-            q_copy(pos, band_of(pos // NZ, pos % NZ)).start()
+        g_t[80:PACK, keys] = both
+        return both
+
+    def backward(i, c):
+        n = NZ - 1 - i
+        keys = pl.ds(pl.multiple_of(n * GROUP, GROUP), GROUP)
+        score_grad(keys)
+        dq[...] += dot(k_t[:, keys], ds_s[...])
+        both = key_grads(keys)
+        row = jnp.where(n == 1, 1, 5 - n)
+        for d in range(NX):
+            pos = n * NX + d
+            send_kv[pos] = both[:, d * TOK : (d + 1) * TOK]
+            kv_copy(pos, band_of(d, row)).start()
+        return c
+
+    lax.fori_loop(0, 1, backward, 0)
+    relay_x(1)
+    lax.fori_loop(1, NZ - 1, backward, 0)
+    keys = slice(0, GROUP)
+    score_grad(keys)
+    for n in range(NZ - 1, -1, -1):
+        cols = slice(n * GROUP, (n + 1) * GROUP)
+        block = (dq[:, cols] + dot(k_t[:, keys], ds_s[:, cols])) * (HD**-0.5)
+        block = jnp.concatenate([block, jnp.zeros((8, GROUP), F32)], axis=0).astype(BF16)
+        g_t[0:80, cols] = block
+        for d in range(NX):
+            pos = n * NX + d
+            send_q[pos] = block[:, d * TOK : (d + 1) * TOK]
+            if pos > 0:
+                q_copy(pos, band_of(d, ORDER[n])).start()
+    both = key_grads(keys)
+    for d in range(NX):
+        send_kv[d] = both[:, d * TOK : (d + 1) * TOK]
+        if d > 0:
+            kv_copy(d, band_of(d, 0)).start()
     recv_kv[me] = send_kv[0]
     recv_q[me] = send_q[0]
 
-    for pos in range(SEQS):
-        cols = slice(pos * TOK, (pos + 1) * TOK)
-        g_t[0:80, cols] = send_q[pos]
-        g_t[80:PACK, cols] = send_kv[pos]
-    for r in (1, 3, 2):
-        side[r][0].wait_recv()
-        side[r][1].wait_recv()
-    side[0][0].wait_recv()
-    side[0][1].wait_recv()
-    far[2].wait_recv()
-    far[3].wait_recv()
+    for n in (1, 2):
+        side[n][0].wait_recv()
+        side[n][1].wait_recv()
+    far_up.wait_recv()
+    far_down.wait_recv()
+    for copy in relays[1]:
+        copy.wait_recv()
     for n in range(3):
         lanes = slice(n * WIN, (n + 1) * WIN)
-        acc = jnp.zeros((PACK, WIN), F32)
-        for d in range(NX):
-            acc = acc + dot(
-                g_t[:, d * 512 : (d + 1) * 512], nall[d, :, :, lanes].reshape(NZ * TOK, WIN)
-            )
+        acc = dot(g_t[...], nall[:, :, :, lanes].reshape(SEQS * TOK, WIN))
         acc = jnp.concatenate([acc[0:HD], acc[80:PACK], jnp.zeros((40, WIN), F32)], axis=0)
         gw[lanes, :] = jnp.transpose(acc)
-    for b in range(reps):
-        block = gw[b * HD : (b + 1) * HD, :]
-        send_w[b] = jnp.concatenate([block, jnp.zeros((8, 256), F32)], axis=0).astype(BF16)
-
-    def w_copy_to(i):
-        return remote(send_w.at[i], recv_w.at[mine], ws_sem.at[i], wr_sem.at[mine], rep_at(i))
-
-    def start_w(i, c):
-        w_copy_to(lax.rem(mine + i, reps)).start()
-        return c
-
-    lax.fori_loop(1, reps, start_w, 0)
-    recv_w[mine] = send_w[mine]
+
+    def w_rows(b):
+        return pl.ds(pl.multiple_of(b * HD, 8), HD)
+
+    spare = jnp.zeros((8, 256), F32)
+    for k in range(chips):
+        block = gw[w_rows(2 * k + 1 - core), :]
+        send_p[k] = jnp.concatenate([block, spare], axis=0).astype(BF16)
+    pair_copy = remote(send_p, recv_p, ps_sem, pr_sem, partner)
+    pair_copy.start()
 
     def wait_kv(i, c):
         other = lax.rem(me + i, SEQS)
@@ -486,6 +528,22 @@
         g_all[D + h * HD : D + (h + 2) * HD, :] = pair.astype(BF16)
         pair = jnp.concatenate([one[HD : 2 * HD], two[HD : 2 * HD]], axis=0)
         g_all[2 * D + h * HD : 2 * D + (h + 2) * HD, :] = pair.astype(BF16)
+
+    def w_copy_to(k):
+        return remote(send_w.at[k], recv_w.at[chip], ws_sem.at[k], wr_sem.at[chip], chip_at(k))
+
+    pair_copy.wait_recv()
+    for k in range(chips):
+        block = gw[w_rows(2 * k + core), :] + recv_p[k].astype(F32)[0:HD]
+        send_w[k] = jnp.concatenate([block, spare], axis=0).astype(BF16)
+
+    def start_w(i, c):
+        w_copy_to(lax.rem(chip + i, chips)).start()
+        return c
+
+    lax.fori_loop(1, chips, start_w, 0)
+    recv_w[chip] = send_w[chip]
+
     normed_grad = dot(w_all[:, D : 3 * D], g_all[D : 3 * D, :])
     lax.fori_loop(1, SEQS, wait_q, 0)
     for h in range(0, SEQS, 2):
@@ -502,21 +560,22 @@
     hgrad_out.start()
 
     def wait_w(i, c):
-        other = lax.rem(mine + i, reps)
+        other = lax.rem(chip + i, chips)
         remote(
-            send_w.at[0], recv_w.at[other], ws_sem.at[0], wr_sem.at[other], rep_at(other)
+            send_w.at[0], recv_w.at[other], ws_sem.at[0], wr_sem.at[other], chip_at(other)
         ).wait_recv()
         return c
 
-    lax.fori_loop(1, reps, wait_w, 0)
+    lax.fori_loop(1, chips, wait_w, 0)
     total = recv_w[0].astype(F32)
-    for b in range(1, reps):
-        total = total + recv_w[b].astype(F32)
+    for k in range(1, chips):
+        total = total + recv_w[k].astype(F32)
     wgrad[...] = total[0:HD, 0 : 3 * HD]
     wgrad_out = pltpu.make_async_copy(wgrad, wgrad_h, out_sem.at[2])
     wgrad_out.start()
 
-    for copy in (halo_up, halo_down, across) + near + far:
+    zs = (up_lo, up_hi, down_hi, down_lo, pass_lo, pass_hi, far_up, far_down)
+    for copy in (halo_up, halo_down, pair_copy) + zs + relays[0] + relays[1]:
         copy.wait_send()
     for pair in side:
         pair[0].wait_send()
@@ -530,11 +589,11 @@
         return c
 
     def drain_w(i, c):
-        w_copy_to(lax.rem(mine + i, reps)).wait_send()
+        w_copy_to(lax.rem(chip + i, chips)).wait_send()
         return c
 
     lax.fori_loop(1, SEQS, drain, 0)
-    lax.fori_loop(1, reps, drain_w, 0)
+    lax.fori_loop(1, chips, drain_w, 0)
     att_out.wait()
     hgrad_out.wait()
     wgrad_out.wait()
@@ -606,8 +665,9 @@
             pltpu.VMEM((NX, NZ, PACK, TOK), BF16),
             pltpu.VMEM((D, 3 * D), BF16),
             pltpu.VMEM((NX, NZ, TOK, D), BF16),
-            pltpu.VMEM((NQ, 2048, QB), BF16),
-            pltpu.VMEM((2048, QB), F32),
+            pltpu.VMEM((2048, 2048), BF16),
+            pltpu.VMEM((2048, 2048), F32),
+            pltpu.VMEM((NZ, 8, GROUP), F32),
             pltpu.VMEM((HD, 2048), BF16),
             pltpu.VMEM((HD, 2048), BF16),
             pltpu.VMEM((HD + 8, 2048), BF16),
@@ -617,8 +677,9 @@
             pltpu.VMEM((HD, 2048), F32),
             pltpu.VMEM((HD, 2048), BF16),
             pltpu.VMEM((2048, HD), BF16),
-            pltpu.VMEM((NQ, 8, QB), F32),
+            pltpu.VMEM((8, 2048), F32),
             pltpu.VMEM((HD, 2048), F32),
+            pltpu.VMEM((GROUP, 2048), BF16),
             pltpu.VMEM((SEQS, 2 * HD, TOK), BF16),
             pltpu.VMEM((SEQS, HD + 8, TOK), BF16),
             pltpu.VMEM((SEQS, 2 * HD, TOK), BF16),
@@ -626,8 +687,10 @@
             pltpu.VMEM((PACK, 2048), BF16),
             pltpu.VMEM((3 * D, TOK), BF16),
             pltpu.VMEM((D, 256), F32),
-            pltpu.VMEM((reps, HD + 8, 256), BF16),
-            pltpu.VMEM((reps, HD + 8, 256), BF16),
+            pltpu.VMEM((reps // 2, HD + 8, 256), BF16),
+            pltpu.VMEM((reps // 2, HD + 8, 256), BF16),
+            pltpu.VMEM((reps // 2, HD + 8, 256), BF16),
+            pltpu.VMEM((reps // 2, HD + 8, 256), BF16),
             pltpu.VMEM((VIEWS, ROWS, COLS, HD), BF16),
             pltpu.VMEM((TOK, D), BF16),
             pltpu.VMEM((D // reps, 3 * HD), F32),
@@ -640,12 +703,16 @@
             DMA((NZ, NX)),
             DMA((NZ, NX)),
             DMA((NZ, NX)),
+            DMA((4,)),
+            DMA((4,)),
             DMA((SEQS,)),
             DMA((SEQS,)),
             DMA((SEQS,)),
             DMA((SEQS,)),
-            DMA((reps,)),
-            DMA((reps,)),
+            DMA,
+            DMA,
+            DMA((reps // 2,)),
+            DMA((reps // 2,)),
         ],
         compiler_params=pltpu.CompilerParams(
             collective_id=0, has_side_effects=True, vmem_limit_bytes=62 * 2**20
@@ -669,8 +736,9 @@
         hand_out,
         out_shape=outs,
         in_specs=[ANY] * 3,
-        out_specs=(ANY,) * 3,
+        out_specs=(pl.BlockSpec(memory_space=pltpu.VMEM),) * 3,
         scratch_shapes=[DMA((3,))],
+        compiler_params=pltpu.CompilerParams(vmem_limit_bytes=62 * 2**20),
         name="hand_out",
     )(*results)
     return (

time: 125 us -> 85 us (0.68)
  the two profiles are of different devices: /device:TPU:57 before, /device:TPU:4 now
where the time goes in v3:
time: 85 us; the launch traced here: 84.1 us
  Pallas kernels  82.7 us (97%)
  between operations  1.45 us (2%)
    pallas_call x1, Pallas kernels, on_device(): pl.pallas_call(functools.partial(layer_kernel, groups, datas), out_shape=...  80.6 us
    pallas_call x1, Pallas kernels, on_device(): pl.pallas_call(hand_out, out_shape=outs, in_specs=[ANY] * 3, out_specs=(p...  2.06 us

profile of v3, /device:TPU:4, one launch (start us, length us, event | category | flops | bytes accessed | tf_op | source)
XLA Modules:
  0.0 84.1 jit_solution(3540039315171304828)
XLA Ops:
  1.3 80.6 %layer.1 = (bf16[8,16,16,72]{3,2,1,0:T(8,128)(2,1)}, bf16[128,1152]{1,0:T(8,128)(2,1)}, f32[72,216]{1,0:T(8,128)}) custom-call(bf16[128,512]{1,0:T(8,128)(2,1)} %bitcast.18, bf16[9,4,512]{2,1,0:T(4,128)(2,1)} %bitcast.19, f32[4]{0:T(128)} %bias_h.1, bf16[8,4,16]{2,1,0:T(4,128)(2,1)} %bitcast.20, s32[1]{0:T(128)S(6)} %copy.17.tstep_h, s32[1,8]{1,0:T(1,128)} %cam_h.1, ...), custom_call_target="tpu_custom_call" | custom-call | tf_op jit(solution)/shard_map/layer/pallas_call | solution.py:641
  81.9 2.1 %hand_out.1 = (bf16[8,16,16,72]{3,2,1,0:T(8,128)(2,1)}, bf16[128,1152]{1,0:T(8,128)(2,1)}, f32[72,216]{1,0:T(8,128)}) custom-call(bf16[8,16,16,72]{3,2,1,0:T(8,128)(2,1)} %get-tuple-element.9.refs_0_, bf16[128,1152]{1,0:T(8,128)(2,1)} %get-tuple-element.10.refs_1_, f32[72,216]{1,0:T(8,128)} %get-tuple-element.11.refs_2_), custom_call_target="tpu_custom_call" | custom-call | tf_op jit(solution)/shard_map/hand_out/pallas_call | solution.py:735

commit v4 on v3

--- a/solution.py
+++ b/solution.py
@@ -484,16 +484,24 @@
     recv_kv[me] = send_kv[0]
     recv_q[me] = send_q[0]
 
-    for n in (1, 2):
-        side[n][0].wait_recv()
-        side[n][1].wait_recv()
+    def partial_w(first, last, lanes):
+        tokens = nall[first:last, :, :, lanes].reshape((last - first) * GROUP, WIN)
+        return dot(g_t[:, first * GROUP : last * GROUP], tokens)
+
+    side[1][0].wait_recv()
+    side[1][1].wait_recv()
     far_up.wait_recv()
+    for n in range(3):
+        lanes = slice(n * WIN, (n + 1) * WIN)
+        s_all[0:PACK, lanes] = partial_w(0, 2, lanes)
+    side[2][0].wait_recv()
+    side[2][1].wait_recv()
     far_down.wait_recv()
     for copy in relays[1]:
         copy.wait_recv()
     for n in range(3):
         lanes = slice(n * WIN, (n + 1) * WIN)
-        acc = dot(g_t[...], nall[:, :, :, lanes].reshape(SEQS * TOK, WIN))
+        acc = s_all[0:PACK, lanes] + partial_w(2, 4, lanes)
         acc = jnp.concatenate([acc[0:HD], acc[80:PACK], jnp.zeros((40, WIN), F32)], axis=0)
         gw[lanes, :] = jnp.transpose(acc)
 
@@ -520,6 +528,21 @@
             send_q.at[0], recv_q.at[other], qs_sem.at[0], qr_sem.at[other], {"seq": other}
         ).wait_recv()
         return c
+
+    def w_copy_to(k):
+        return remote(send_w.at[k], recv_w.at[chip], ws_sem.at[k], wr_sem.at[chip], chip_at(k))
+
+    pair_copy.wait_recv()
+    for k in range(chips):
+        block = gw[w_rows(2 * k + core), :] + recv_p[k].astype(F32)[0:HD]
+        send_w[k] = jnp.concatenate([block, spare], axis=0).astype(BF16)
+
+    def start_w(i, c):
+        w_copy_to(lax.rem(chip + i, chips)).start()
+        return c
+
+    lax.fori_loop(1, chips, start_w, 0)
+    recv_w[chip] = send_w[chip]
 
     lax.fori_loop(1, SEQS, wait_kv, 0)
     for h in range(0, SEQS, 2):
@@ -528,21 +551,6 @@
         g_all[D + h * HD : D + (h + 2) * HD, :] = pair.astype(BF16)
         pair = jnp.concatenate([one[HD : 2 * HD], two[HD : 2 * HD]], axis=0)
         g_all[2 * D + h * HD : 2 * D + (h + 2) * HD, :] = pair.astype(BF16)
-
-    def w_copy_to(k):
-        return remote(send_w.at[k], recv_w.at[chip], ws_sem.at[k], wr_sem.at[chip], chip_at(k))
-
-    pair_copy.wait_recv()
-    for k in range(chips):
-        block = gw[w_rows(2 * k + core), :] + recv_p[k].astype(F32)[0:HD]
-        send_w[k] = jnp.concatenate([block, spare], axis=0).astype(BF16)
-
-    def start_w(i, c):
-        w_copy_to(lax.rem(chip + i, chips)).start()
-        return c
-
-    lax.fori_loop(1, chips, start_w, 0)
-    recv_w[chip] = send_w[chip]
 
     normed_grad = dot(w_all[:, D : 3 * D], g_all[D : 3 * D, :])
     lax.fori_loop(1, SEQS, wait_q, 0)

time: 85 us -> 84.4 us (level)
  Pallas kernels: 82.7 us -> 81.3 us
    pallas_call x1, Pallas kernels: 80.6 us -> 79.2 us  [on_device(): pl.pallas_call(functools.partial(layer_kernel, groups, datas), out_shape=...]
where the time goes in v4:
time: 84.4 us; the launch traced here: 82.7 us
  Pallas kernels  81.3 us (96%)
  between operations  1.45 us (2%)
    pallas_call x1, Pallas kernels, on_device(): pl.pallas_call(functools.partial(layer_kernel, groups, datas), out_shape=...  79.2 us
    pallas_call x1, Pallas kernels, on_device(): pl.pallas_call(hand_out, out_shape=outs, in_specs=[ANY] * 3, out_specs=(p...  2.06 us

profile of v4, /device:TPU:4, one launch (start us, length us, event | category | flops | bytes accessed | tf_op | source)
XLA Modules:
  0.0 82.7 jit_solution(6979866374372400815)
XLA Ops:
  1.3 79.2 %layer.1 = (bf16[8,16,16,72]{3,2,1,0:T(8,128)(2,1)}, bf16[128,1152]{1,0:T(8,128)(2,1)}, f32[72,216]{1,0:T(8,128)}) custom-call(bf16[128,512]{1,0:T(8,128)(2,1)} %bitcast.18, bf16[9,4,512]{2,1,0:T(4,128)(2,1)} %bitcast.19, f32[4]{0:T(128)} %bias_h.1, bf16[8,4,16]{2,1,0:T(4,128)(2,1)} %bitcast.20, s32[1]{0:T(128)S(6)} %copy.17.tstep_h, s32[1,8]{1,0:T(1,128)} %cam_h.1, ...), custom_call_target="tpu_custom_call" | custom-call | tf_op jit(solution)/shard_map/layer/pallas_call | solution.py:649
  80.5 2.1 %hand_out.1 = (bf16[8,16,16,72]{3,2,1,0:T(8,128)(2,1)}, bf16[128,1152]{1,0:T(8,128)(2,1)}, f32[72,216]{1,0:T(8,128)}) custom-call(bf16[8,16,16,72]{3,2,1,0:T(8,128)(2,1)} %get-tuple-element.9.refs_0_, bf16[128,1152]{1,0:T(8,128)(2,1)} %get-tuple-element.10.refs_1_, f32[72,216]{1,0:T(8,128)} %get-tuple-element.11.refs_2_), custom_call_target="tpu_custom_call" | custom-call | tf_op jit(solution)/shard_map/hand_out/pallas_call | solution.py:743
